TPU v7x, 32 devices: a whole 2x2x4 slice. The times are simulated.
32 devices in a mesh: ctx: 8 (over z, x), tp: 4 (over y, core).
Axes of the slice: x: 2, y: 2, z: 4, core: 2. Of those that a mesh axis runs over, the one named last changes fastest.
Arguments:
- tokens: bfloat16 [2048, 4096], P(('ctx', 'tp')), may hold values from -6 to 6
- in_x: bfloat16 [4096, 4096], P(None, 'tp'), may hold values from -0.09375 to 0.09375
- in_bc: bfloat16 [4096, 256], replicated, may hold values from -0.09375 to 0.09375
- in_dt: bfloat16 [4096, 64], P(None, 'tp'), may hold values from -0.09375 to 0.09375
- conv_x: float32 [4, 4096], P(None, 'tp'), may hold values from -3 to 3
- conv_bc: float32 [4, 256], replicated, may hold values from -3 to 3
- dt_bias: float32 [64], P('tp'), may hold values from -7.5 to -3.5
- a_log: float32 [64], P('tp'), may hold values from -4.61 to 0.41
- skip_d: float32 [64], P('tp'), may hold values from 0.5 to 1.5
- norm_gain: float32 [4096], P('tp'), may hold values from 0.1 to 1.9
- out_w: bfloat16 [4096, 4096], P('tp'), may hold values from -0.09375 to 0.09375
Outputs:
- mixed: bfloat16 [2048, 4096], P(('ctx', 'tp'))
All inputs are finite; a program needn't handle non-finite values.
Results may differ from a plain program's by a relative error of at most 0.019.
Values may be sent and summed in bfloat16 or wider, within the bound.
A program may use at most 64 MiB of HBM per device.

v0:
```python
import jax
import jax.numpy as jnp
from jax import lax
from jax.sharding import PartitionSpec as P

BLOCK = 256


def passed_along(shard, axis, by):
    devices = lax.axis_size(axis)
    pairs = [(i, i + by) for i in range(devices) if 0 <= i + by < devices]
    return lax.ppermute(shard, axis, pairs)


def causal_conv(prev, cur, kernel):
    ext = jnp.concatenate([prev, cur], 0).astype(jnp.float32)
    rows = cur.shape[0]
    taps = kernel.shape[0]
    total = kernel[0][None, :] * ext[0:rows]
    for k in range(1, taps):
        total = total + kernel[k][None, :] * ext[k : k + rows]
    return jax.nn.silu(total)


def ssd_block(state, xb, bb, cb, lab, dtb):
    hi = lax.Precision.HIGHEST
    length = lab.shape[0]
    cs = jnp.cumsum(lab, axis=0)
    cs_heads = cs.T
    scores = jnp.dot(cb, bb.T, precision=hi)
    diff = cs_heads[:, :, None] - cs_heads[:, None, :]
    later = lax.broadcasted_iota(jnp.int32, (length, length), 0)
    earlier = lax.broadcasted_iota(jnp.int32, (length, length), 1)
    tri = (later >= earlier)[None, :, :]
    decay = jnp.exp(jnp.where(tri, diff, -jnp.inf))
    xdt = xb * dtb[:, :, None]
    weighted = scores[None, :, :] * decay
    y_in = jnp.einsum("hts,shp->thp", weighted, xdt, precision=hi)
    y_st = jnp.exp(cs)[:, :, None] * jnp.einsum("tn,hpn->thp", cb, state, precision=hi)
    tail = jnp.exp(cs[-1][None, :] - cs)
    fresh = jnp.einsum("shp,sn->hpn", xdt * tail[:, :, None], bb, precision=hi)
    new_state = jnp.exp(cs[-1])[:, None, None] * state + fresh
    return (new_state, y_in + y_st, cs)


def per_device(
    tokens, in_x, in_bc, in_dt, conv_x, conv_bc, dt_bias, a_log, skip_d, norm_gain, out_w
):
    hi = lax.Precision.HIGHEST
    gathered = lax.all_gather(tokens, "tp", axis=0, tiled=True)
    bc_raw = jnp.dot(gathered, in_bc, preferred_element_type=jnp.float32).astype(jnp.bfloat16)
    x_raw = jnp.dot(gathered, in_x, preferred_element_type=jnp.float32).astype(jnp.bfloat16)
    dt_raw = jnp.dot(gathered, in_dt, preferred_element_type=jnp.float32)
    span_rows = gathered.shape[0]
    margin = conv_x.shape[0] - 1
    prev_x, prev_bc = passed_along(
        (x_raw[span_rows - margin :], bc_raw[span_rows - margin :]), "ctx", 1
    )
    x_conv = causal_conv(prev_x, x_raw, conv_x)
    bc_conv = causal_conv(prev_bc, bc_raw, conv_bc)
    states = in_bc.shape[1] // 2
    b_all = bc_conv[:, :states]
    c_all = bc_conv[:, states:]
    heads_here = a_log.shape[0]
    head_width = x_conv.shape[1] // heads_here
    step_dt = jax.nn.softplus(dt_raw + dt_bias[None, :])
    log_decay = -jnp.exp(a_log)[None, :] * step_dt
    blocks = span_rows // BLOCK

    def scan_step(carry, inputs):
        state, offset = carry
        xb, bb, cb, lab, dtb = inputs
        new_state, y_blk, cs = ssd_block(state, xb, bb, cb, lab, dtb)
        return ((new_state, offset + cs[-1]), (y_blk, cs + offset[None, :]))

    start = (
        jnp.zeros((heads_here, head_width, states), jnp.float32),
        jnp.zeros((heads_here,), jnp.float32),
    )
    (end_state, total_log), (y_blocks, cum_blocks) = lax.scan(
        scan_step,
        start,
        (
            x_conv.reshape(blocks, BLOCK, heads_here, head_width),
            b_all.reshape(blocks, BLOCK, states),
            c_all.reshape(blocks, BLOCK, states),
            log_decay.reshape(blocks, BLOCK, heads_here),
            step_dt.reshape(blocks, BLOCK, heads_here),
        ),
    )
    span_decay = jnp.exp(total_log)

    def relay(turn, incoming):
        outgoing = span_decay[:, None, None] * incoming + end_state
        return passed_along(outgoing, "ctx", 1)

    entering = lax.fori_loop(0, lax.axis_size("ctx") - 1, relay, jnp.zeros_like(end_state))
    cum_all = cum_blocks.reshape(span_rows, heads_here)
    x_flat = x_conv.reshape(span_rows, heads_here, head_width)
    carried = jnp.exp(cum_all)[:, :, None] * jnp.einsum(
        "tn,hpn->thp", c_all, entering, precision=hi
    )
    y_all = (
        y_blocks.reshape(span_rows, heads_here, head_width)
        + carried
        + skip_d[None, :, None] * x_flat
    )
    mean_sq = jnp.mean(y_all * y_all, axis=-1, keepdims=True)
    normed = (
        (y_all * lax.rsqrt(mean_sq + 1e-05) * norm_gain.reshape(heads_here, head_width)[None])
        .reshape(span_rows, heads_here * head_width)
        .astype(jnp.bfloat16)
    )
    return lax.psum_scatter(
        jnp.dot(normed, out_w, preferred_element_type=jnp.float32).astype(jnp.bfloat16),
        "tp",
        scatter_dimension=0,
        tiled=True,
    )


def solution(mesh):
    return jax.shard_map(
        per_device,
        mesh=mesh,
        in_specs=(
            P(("ctx", "tp"), None),
            P(None, "tp"),
            P(),
            P(None, "tp"),
            P(None, "tp"),
            P(),
            P("tp"),
            P("tp"),
            P("tp"),
            P("tp"),
            P("tp", None),
        ),
        out_specs=P(("ctx", "tp"), None),
        check_vma=False,
    )
```

profile of v0, /device:TPU:31, one launch (start us, length us, event | category | flops | bytes accessed | tf_op | source)
XLA Modules:
  0.0 214.3 jit_solution(770629602176578218)
XLA Ops:
  6.5 0.0 copy-start
  6.5 0.0 all-gather.2.cloned.1.call-start
  6.5 0.7 all-gather.2.cloned.1.call-update
  7.3 0.0 reduce-scatter.2.cloned.1.call-start
  7.3 0.8 mul.245
  8.1 0.7 exponential_negate_fusion
  8.8 0.8 fusion.48
  9.6 0.9 fusion.47
  10.5 21.4 %all-gather.2.cloned.1.call-done = bf16[256,4096]{1,0:T(8,128)(2,1)} async-done(((bf16[64,4096]{1,0:T(8,128)(2,1)}), bf16[256,4096]{1,0:T(8,128)(2,1)}) %all-gather.2.cloned.1.call-update) | async-done | bytes 2097168 | tf_op jit(solution)/shard_map/all_gather | solution.py:50
  31.9 2.3 %compare_select_fusion.1 = (f32[256,16]{0,1:T(8,128)S(1)}, f32[256,16]{0,1:T(8,128)S(1)}) fusion(f32[16]{0:T(128)} %param.19, bf16[256,4096]{1,0:T(8,128)(2,1)} %all-gather.2.cloned.1.call-done, bf16[4096,16]{0,1:T(8,128)(2,1)} %param.16), kind=kOutput, calls=%fused_computation.60 | convolution fusion | flops 33583104 | bytes 2261056 | tf_op jit(solution)/shard_map/dot_general | solution.py:53
  34.3 0.1 copy_bitcast_fusion.1
  34.4 0.6 reduce-window.6
  34.9 0.2 slice_reduce_fusion
  35.1 0.7 fusion.46
  35.8 0.2 slice_reduce_fusion.1
  36.0 0.1 subtract_exponential_fusion
  36.1 0.0 copy-done
  36.1 0.0 copy-start.1
  36.1 2.4 %convolution_convert_fusion.2 = bf16[256,256]{1,0:T(8,128)(2,1)S(1)} fusion(bf16[256,4096]{1,0:T(8,128)(2,1)} %all-gather.2.cloned.1.call-done, bf16[4096,256]{1,0:T(8,128)(2,1)S(1)} %copy-done), kind=kOutput, calls=%fused_computation.20 | convolution fusion | flops 536936448 | bytes 4325376 | tf_op jit(solution)/shard_map/dot_general | solution.py:51
  38.6 1.3 collective-permute-start.2
  39.9 0.0 copy-done.1
  39.9 5.8 %convolution_convert_fusion.1 = bf16[256,1024]{1,0:T(8,128)(2,1)S(1)} fusion(bf16[256,4096]{1,0:T(8,128)(2,1)S(1)} %copy-done.1, bf16[4096,1024]{1,0:T(8,128)(2,1)} %param.14), kind=kOutput, calls=%fused_computation.18 | convolution fusion | flops 2147745792 | bytes 11010048 | tf_op jit(solution)/shard_map/dot_general | solution.py:52
  45.7 1.5 collective-permute-start.1
  47.2 0.0 collective-permute-done.2
  47.2 0.2 divide_multiply_fusion.1
  47.4 1.1 fusion.33
  48.5 2.2 %collective-permute-done.1 = bf16[3,1024]{1,0:T(4,128)(2,1)S(1)} collective-permute-done((bf16[3,1024]{1,0:T(4,128)(2,1)S(1)}, bf16[3,1024]{1,0:T(4,128)(2,1)S(1)}, u32[]{:S(2)}, u32[]{:S(2)}) %collective-permute-start.1) | collective-permute-done | bytes 6176 | tf_op jit(solution)/shard_map/ppermute | solution.py:12
  50.7 0.1 maximum_convert_fusion
  50.9 0.6 divide_multiply_fusion
  51.5 0.0 copy-start.2
  51.5 1.3 copy.22
  52.8 2.2 %convolution_add_fusion = f32[16,64,128]{2,1,0:T(8,128)S(1)} fusion(f32[256,16,64]{0,2,1:T(8,128)} %bitcast.69, f32[256,16]{0,1:T(8,128)S(1)} %get-tuple-element.66, f32[256,16]{0,1:T(8,128)S(1)} %get-tuple-element.80, f32[16]{0:T(128)S(1)} %get-tuple-element.78, f32[256,256]{1,0:T(8,128)S(1)} %divide_multiply_fusion.1), kind=kOutput, calls=%fused_computation.19 | convolution fusion | flops 403308544 | bytes 1737216 | tf_op jit(solution)/shard_map/while/body/eval_jaxpr/shp,sn->hpn/dot_general | solution.py:41
  55.0 0.0 copy-done.2
  55.0 6.0 %fusion.10 = f32[256,16,64]{0,2,1:T(8,128)S(1)} fusion(f32[16,256]{1,0:T(8,128)S(1)} %copy-done.2, f32[256,256]{1,0:T(8,128)} %fusion.33, pred[256,256]{1,0:T(8,128)(4,1)S(1)} %iota_compare_fusion, f32[256,16,64]{0,2,1:T(8,128)} %bitcast.70, f32[256,16]{0,1:T(8,128)S(1)} %get-tuple-element.80), kind=kOutput, calls=%fused_computation.12 | convolution fusion | flops 808714240 | bytes 2457600 | tf_op jit(solution)/shard_map/while/body/eval_jaxpr/hts,shp->thp/dot_general | solution.py:38
  61.1 2.0 fusion.15
  63.1 0.0 copy-start.3
  63.1 93.1 %while.2 = (s32[]{:T(128)}, f32[16,64,128]{2,1,0:T(8,128)S(1)}, f32[16]{0:T(128)S(1)}, f32[16,64,128]{2,1,0:T(8,128)S(1)}, s32[]{:T(128)}) while((s32[]{:T(128)}, f32[16,64,128]{2,1,0:T(8,128)S(1)}, f32[16]{0:T(128)S(1)}, f32[16,64,128]{2,1,0:T(8,128)S(1)}, s32[]{:T(128)}) %tuple.31), condition=%wide.region_3.4_spmd, body=%wide.region_2.3_spmd.sunk | while | flops 262146 | bytes 3670181 | solution.py:97
  63.1 0.9 multiply_add_fusion.2
  64.1 1.3 collective-permute-start
  65.3 13.7 %collective-permute-done = f32[16,64,128]{2,1,0:T(8,128)S(1)} collective-permute-done((f32[16,64,128]{2,1,0:T(8,128)}, f32[16,64,128]{2,1,0:T(8,128)S(1)}, u32[]{:S(2)}, u32[]{:S(2)}) %collective-permute-start) | collective-permute-done | bytes 524320 | tf_op jit(solution)/shard_map/while/body/eval_jaxpr/ppermute | solution.py:12
  79.0 0.9 multiply_add_fusion.2
  79.9 1.3 collective-permute-start
  81.2 12.5 %collective-permute-done = f32[16,64,128]{2,1,0:T(8,128)S(1)} collective-permute-done((f32[16,64,128]{2,1,0:T(8,128)}, f32[16,64,128]{2,1,0:T(8,128)S(1)}, u32[]{:S(2)}, u32[]{:S(2)}) %collective-permute-start) | collective-permute-done | bytes 524320 | tf_op jit(solution)/shard_map/while/body/eval_jaxpr/ppermute | solution.py:12
  93.7 0.9 multiply_add_fusion.2
  94.6 1.3 collective-permute-start
  95.9 11.6 %collective-permute-done = f32[16,64,128]{2,1,0:T(8,128)S(1)} collective-permute-done((f32[16,64,128]{2,1,0:T(8,128)}, f32[16,64,128]{2,1,0:T(8,128)S(1)}, u32[]{:S(2)}, u32[]{:S(2)}) %collective-permute-start) | collective-permute-done | bytes 524320 | tf_op jit(solution)/shard_map/while/body/eval_jaxpr/ppermute | solution.py:12
  107.5 0.9 multiply_add_fusion.2
  108.4 1.3 collective-permute-start
  109.7 10.6 %collective-permute-done = f32[16,64,128]{2,1,0:T(8,128)S(1)} collective-permute-done((f32[16,64,128]{2,1,0:T(8,128)}, f32[16,64,128]{2,1,0:T(8,128)S(1)}, u32[]{:S(2)}, u32[]{:S(2)}) %collective-permute-start) | collective-permute-done | bytes 524320 | tf_op jit(solution)/shard_map/while/body/eval_jaxpr/ppermute | solution.py:12
  120.3 0.9 multiply_add_fusion.2
  121.2 1.3 collective-permute-start
  122.5 9.5 %collective-permute-done = f32[16,64,128]{2,1,0:T(8,128)S(1)} collective-permute-done((f32[16,64,128]{2,1,0:T(8,128)}, f32[16,64,128]{2,1,0:T(8,128)S(1)}, u32[]{:S(2)}, u32[]{:S(2)}) %collective-permute-start) | collective-permute-done | bytes 524320 | tf_op jit(solution)/shard_map/while/body/eval_jaxpr/ppermute | solution.py:12
  132.0 0.9 multiply_add_fusion.2
  132.9 1.3 collective-permute-start
  134.2 9.7 %collective-permute-done = f32[16,64,128]{2,1,0:T(8,128)S(1)} collective-permute-done((f32[16,64,128]{2,1,0:T(8,128)}, f32[16,64,128]{2,1,0:T(8,128)S(1)}, u32[]{:S(2)}, u32[]{:S(2)}) %collective-permute-start) | collective-permute-done | bytes 524320 | tf_op jit(solution)/shard_map/while/body/eval_jaxpr/ppermute | solution.py:12
  143.9 0.9 multiply_add_fusion.2
  144.8 1.3 collective-permute-start
  146.1 10.1 %collective-permute-done = f32[16,64,128]{2,1,0:T(8,128)S(1)} collective-permute-done((f32[16,64,128]{2,1,0:T(8,128)}, f32[16,64,128]{2,1,0:T(8,128)S(1)}, u32[]{:S(2)}, u32[]{:S(2)}) %collective-permute-start) | collective-permute-done | bytes 524320 | tf_op jit(solution)/shard_map/while/body/eval_jaxpr/ppermute | solution.py:12
  156.3 0.0 copy-done.3
  156.3 2.6 %multiply_reduce_fusion = (f32[256,16]{0,1:T(8,128)S(1)}, f32[256,16,64]{0,2,1:T(8,128)S(1)}) fusion(f32[256,16,64]{0,2,1:T(8,128)} %bitcast.71, f32[16]{0:T(128)S(1)} %copy-done.3, f32[256,16,64]{0,2,1:T(8,128)} %fusion.15, f32[16,64,128]{2,1,0:T(8,128)S(1)} %get-tuple-element.51, f32[256,256]{1,0:T(8,128)S(1)} %divide_multiply_fusion.1, ...), kind=kOutput, calls=%fused_computation.30 | convolution fusion | flops 404221952 | bytes 3834368 | tf_op jit(solution)/shard_map/tn,hpn->thp/dot_general | solution.py:100
  158.9 0.2 multiply_convert_fusion
  159.1 7.1 %convolution_convert_fusion = bf16[256,4096]{1,0:T(8,128)(2,1)} fusion(bf16[256,1024]{0,1:T(8,128)(2,1)S(1)} %bitcast.72, bf16[1024,4096]{1,0:T(8,128)(2,1)} %param.23), kind=kOutput, calls=%fused_computation.1 | convolution fusion | flops 2148532224 | bytes 11010048 | tf_op jit(solution)/shard_map/dot_general | solution.py:115
  166.2 0.0 reduce-scatter.2.cloned.1.call-update
  166.2 41.2 %reduce-scatter.2.cloned.1.call-done = bf16[64,4096]{1,0:T(8,128)(2,1)} async-done(((bf16[256,4096]{1,0:T(8,128)(2,1)}), bf16[64,4096]{1,0:T(8,128)(2,1)}) %reduce-scatter.2.cloned.1.call-update) | async-done | bytes 524304 | tf_op jit(solution)/shard_map/reduce_scatter | solution.py:114
  (9 shorter events, 0.2 us)
Async XLA Ops:
  6.5 29.5 %copy-start = (bf16[4096,256]{1,0:T(8,128)(2,1)S(1)}, bf16[4096,256]{1,0:T(8,128)(2,1)}, u32[]{:S(2)}) copy-start(bf16[4096,256]{1,0:T(8,128)(2,1)} %param.15) | copy-start | bytes 6291460
  6.5 25.4 %all-gather.2.cloned.1.call-start = ((), (), s32[]{:S(2)}) async-start(), calls=%async_computation.1 | async-start | bytes 2621440 | tf_op jit(solution)/shard_map/all_gather | solution.py:50
  7.3 200.2 %reduce-scatter.2.cloned.1.call-start = ((), (), s32[]{:S(2)}) async-start(), calls=%async_computation.2 | async-start | bytes 2621440 | tf_op jit(solution)/shard_map/reduce_scatter | solution.py:114
  36.1 3.8 %copy-start.1 = (bf16[256,4096]{1,0:T(8,128)(2,1)S(1)}, bf16[256,4096]{1,0:T(8,128)(2,1)}, u32[]{:S(2)}) copy-start(bf16[256,4096]{1,0:T(8,128)(2,1)} %all-gather.2.cloned.1.call-done) | copy-start | bytes 6291460
  38.6 8.6 %collective-permute-start.2 = (bf16[3,256]{1,0:T(4,128)(2,1)S(1)}, bf16[3,256]{1,0:T(4,128)(2,1)S(1)}, u32[]{:S(2)}, u32[]{:S(2)}) collective-permute-start(bf16[3,256]{1,0:T(4,128)(2,1)S(1)} %slice.100), channel_id=1, source_target_pairs={{0,4},{4,8},{8,12},{12,16},{16,20},{20,24},{24,28},{1,5},{5,9},{9,... | collective-permute-start | bytes 4616 | tf_op jit(solution)/shard_map/ppermute | solution.py:12
  45.7 5.0 %collective-permute-start.1 = (bf16[3,1024]{1,0:T(4,128)(2,1)S(1)}, bf16[3,1024]{1,0:T(4,128)(2,1)S(1)}, u32[]{:S(2)}, u32[]{:S(2)}) collective-permute-start(bf16[3,1024]{1,0:T(4,128)(2,1)S(1)} %slice.95), channel_id=1, source_target_pairs={{0,4},{4,8},{8,12},{12,16},{16,20},{20,24},{24,28},{1,5},{5,9},{9,... | collective-permute-start | bytes 18440 | tf_op jit(solution)/shard_map/ppermute | solution.py:12
  51.5 3.5 %copy-start.2 = (f32[16,256]{1,0:T(8,128)S(1)}, f32[16,256]{1,0:T(8,128)}, u32[]{:S(2)}) copy-start(f32[16,256]{1,0:T(8,128)} %get-tuple-element.69) | copy-start | bytes 49156
  63.1 93.1 %copy-start.3 = (f32[16]{0:T(128)S(1)}, f32[16]{0:T(128)}, u32[]{:S(2)}) copy-start(f32[16]{0:T(128)} %param.21) | copy-start | bytes 196
  64.1 15.0 %collective-permute-start = (f32[16,64,128]{2,1,0:T(8,128)}, f32[16,64,128]{2,1,0:T(8,128)S(1)}, u32[]{:S(2)}, u32[]{:S(2)}) collective-permute-start(f32[16,64,128]{2,1,0:T(8,128)} %multiply_add_fusion.2), channel_id=1, source_target_pairs={{0,4},{4,8},{8,12},{12,16},{16,20},{20,24},{24,28},{1,5},{5,9},{9,... | collective-permute-start | bytes 1572872 | tf_op jit(solution)/shard_map/while/body/eval_jaxpr/ppermute | solution.py:12
  79.9 13.8 %collective-permute-start = (f32[16,64,128]{2,1,0:T(8,128)}, f32[16,64,128]{2,1,0:T(8,128)S(1)}, u32[]{:S(2)}, u32[]{:S(2)}) collective-permute-start(f32[16,64,128]{2,1,0:T(8,128)} %multiply_add_fusion.2), channel_id=1, source_target_pairs={{0,4},{4,8},{8,12},{12,16},{16,20},{20,24},{24,28},{1,5},{5,9},{9,... | collective-permute-start | bytes 1572872 | tf_op jit(solution)/shard_map/while/body/eval_jaxpr/ppermute | solution.py:12
  94.6 12.9 %collective-permute-start = (f32[16,64,128]{2,1,0:T(8,128)}, f32[16,64,128]{2,1,0:T(8,128)S(1)}, u32[]{:S(2)}, u32[]{:S(2)}) collective-permute-start(f32[16,64,128]{2,1,0:T(8,128)} %multiply_add_fusion.2), channel_id=1, source_target_pairs={{0,4},{4,8},{8,12},{12,16},{16,20},{20,24},{24,28},{1,5},{5,9},{9,... | collective-permute-start | bytes 1572872 | tf_op jit(solution)/shard_map/while/body/eval_jaxpr/ppermute | solution.py:12
  108.4 11.9 %collective-permute-start = (f32[16,64,128]{2,1,0:T(8,128)}, f32[16,64,128]{2,1,0:T(8,128)S(1)}, u32[]{:S(2)}, u32[]{:S(2)}) collective-permute-start(f32[16,64,128]{2,1,0:T(8,128)} %multiply_add_fusion.2), channel_id=1, source_target_pairs={{0,4},{4,8},{8,12},{12,16},{16,20},{20,24},{24,28},{1,5},{5,9},{9,... | collective-permute-start | bytes 1572872 | tf_op jit(solution)/shard_map/while/body/eval_jaxpr/ppermute | solution.py:12
  121.2 10.7 %collective-permute-start = (f32[16,64,128]{2,1,0:T(8,128)}, f32[16,64,128]{2,1,0:T(8,128)S(1)}, u32[]{:S(2)}, u32[]{:S(2)}) collective-permute-start(f32[16,64,128]{2,1,0:T(8,128)} %multiply_add_fusion.2), channel_id=1, source_target_pairs={{0,4},{4,8},{8,12},{12,16},{16,20},{20,24},{24,28},{1,5},{5,9},{9,... | collective-permute-start | bytes 1572872 | tf_op jit(solution)/shard_map/while/body/eval_jaxpr/ppermute | solution.py:12
  132.9 11.0 %collective-permute-start = (f32[16,64,128]{2,1,0:T(8,128)}, f32[16,64,128]{2,1,0:T(8,128)S(1)}, u32[]{:S(2)}, u32[]{:S(2)}) collective-permute-start(f32[16,64,128]{2,1,0:T(8,128)} %multiply_add_fusion.2), channel_id=1, source_target_pairs={{0,4},{4,8},{8,12},{12,16},{16,20},{20,24},{24,28},{1,5},{5,9},{9,... | collective-permute-start | bytes 1572872 | tf_op jit(solution)/shard_map/while/body/eval_jaxpr/ppermute | solution.py:12
  144.8 11.4 %collective-permute-start = (f32[16,64,128]{2,1,0:T(8,128)}, f32[16,64,128]{2,1,0:T(8,128)S(1)}, u32[]{:S(2)}, u32[]{:S(2)}) collective-permute-start(f32[16,64,128]{2,1,0:T(8,128)} %multiply_add_fusion.2), channel_id=1, source_target_pairs={{0,4},{4,8},{8,12},{12,16},{16,20},{20,24},{24,28},{1,5},{5,9},{9,... | collective-permute-start | bytes 1572872 | tf_op jit(solution)/shard_map/while/body/eval_jaxpr/ppermute | solution.py:12
Sparse Core Ops, SparseCore 0:
  8.9 22.9 all-gather.1
  166.4 41.0 reduce-scatter.1
where the time goes:
time: 218 us; the launch traced here: 214 us
  waiting for transfers between devices  143 us (66%)
  matrix products  31.6 us (14%)
  between operations  13.6 us (6%)
  starting transfers between devices  11.8 us (5%)
  other arithmetic  9.68 us (4%)
  local copies, waits for them, and re-layouts  4.21 us (2%)
    ppermute x9, waiting for transfers between devices, passed_along(): return lax.ppermute(shard, axis, pairs)  79.9 us
    reduce_scatter x1, waiting for transfers between devices, per_device(): lax.psum_scatter(jnp.dot(normed, out_w, preferred_element_type=jnp.float3...  41.2 us
    all_gather x1, waiting for transfers between devices, per_device(): gathered = lax.all_gather(tokens, 'tp', axis=0, tiled=True)  21.4 us
    ppermute x9, starting transfers between devices, passed_along(): return lax.ppermute(shard, axis, pairs)  11.7 us
    dot_general x1, matrix products, per_device(): jnp.dot(normed, out_w, preferred_element_type=jnp.float32)  7.09 us
    add x7, other arithmetic, relay(): outgoing = span_decay[:, None, None] * incoming + end_state  6.36 us
    dot_general x1, matrix products, ssd_block(): y_in = jnp.einsum('hts,shp->thp', weighted, xdt, precision=hi)  6.02 us
    dot_general x1, matrix products, per_device(): jnp.dot(gathered, in_x, preferred_element_type=jnp.float32)  5.77 us
  transfers between devices with their start and end apart: 11, of which 10 were waited for; matrix products, arithmetic and copies ran while one was open for 5% of the time, Pallas kernels for 0%

commit v1 on v0

v1 whole, which is shorter than its diff:
```python
import functools

import jax
import jax.numpy as jnp
from jax import lax
from jax.experimental import pallas as pl
from jax.experimental.pallas import tpu as pltpu
from jax.sharding import PartitionSpec as P

MESH = pl.DeviceIdType.MESH
F32 = jnp.float32
BF16 = jnp.bfloat16
K_PARTS = 4
OUT_PARTS = 8
TILE = 256
LANES = 128


def dot(a, b):
    return jnp.dot(a, b, preferred_element_type=F32)


def split(v, parts):
    terms = []
    for _ in range(parts):
        term = v.astype(BF16)
        terms.append(term)
        v = v - term.astype(F32)
    return terms


def layer_kernel(
    ctx_size,
    tokens,
    in_x,
    in_bc,
    in_dt,
    out_w,
    conv_x,
    conv_bc,
    dt_bias,
    a_log,
    skip_d,
    gain,
    out,
    gath,
    w_in,
    w_dt,
    w_out,
    acc,
    acc_dt,
    ext,
    taps,
    xc,
    xdt,
    xtail,
    ecs,
    yb,
    score,
    end,
    st_in,
    st_out,
    normed,
    part,
    own,
    send1,
    recv1,
    send2,
    recv2,
    load_sem,
    tok_sem,
    a_send,
    a_recv,
    b_send,
    b_recv,
    f_send,
    f_recv,
    conv_sem,
    s_send,
    s_recv,
    r1_send,
    r1_recv,
    r2_send,
    r2_recv,
):
    c = lax.axis_index("ctx")
    t = lax.axis_index("tp")
    mate = t + 1 - 2 * (t % 2)
    across = (t + 2) % 4
    far = (mate + 2) % 4
    rows, depth = tokens.shape
    span = 4 * rows
    inner = in_x.shape[1]
    bc = in_bc.shape[1]
    wide = inner + bc
    states = bc // 2
    heads = dt_bias.shape[1]
    kc = depth // K_PARTS
    oc = depth // OUT_PARTS
    has_prev = c > 0
    has_next = c < ctx_size - 1

    def cols(i, size):
        return pl.ds(pl.multiple_of(i * size, size), size)

    def load(k):
        ks = cols(k, kc)
        return (
            pltpu.make_async_copy(in_x.at[ks, :], w_in.at[ks, 0:inner], load_sem.at[0, k]),
            pltpu.make_async_copy(in_bc.at[ks, :], w_in.at[ks, inner:wide], load_sem.at[1, k]),
        )

    load_dt = pltpu.make_async_copy(in_dt, w_dt, load_sem.at[2, 0])
    load_out = pltpu.make_async_copy(out_w, w_out, load_sem.at[2, 1])
    load_tok = pltpu.make_async_copy(tokens, gath.at[t], tok_sem)

    def remote(src, dst, send, recv, cc, tt):
        return pltpu.make_async_remote_copy(
            src_ref=src,
            dst_ref=dst,
            send_sem=send,
            recv_sem=recv,
            device_id=(cc, tt),
            device_id_type=MESH,
        )

    def copy_a(k):
        ks = cols(k, kc)
        return remote(
            tokens.at[:, ks], gath.at[t, :, ks], a_send.at[k], a_recv.at[k], c, across
        )

    def copy_b(k):
        ks = cols(k, kc)
        return remote(tokens.at[:, ks], gath.at[t, :, ks], b_send.at[k], b_recv.at[k], c, mate)

    def copy_f(k):
        ks = cols(k, kc)
        return remote(
            gath.at[across, :, ks], gath.at[across, :, ks], f_send.at[k], f_recv.at[k], c, mate
        )

    def got(block, k, send, recv):
        ks = cols(k, kc)
        return remote(
            gath.at[block, :, ks], gath.at[block, :, ks], send.at[k], recv.at[k], c, mate
        )

    barrier = pltpu.get_barrier_semaphore()
    for tt in (mate, across):
        pl.semaphore_signal(barrier, inc=1, device_id=(c, tt), device_id_type=MESH)

    @pl.when(has_prev)
    def _():
        pl.semaphore_signal(barrier, inc=1, device_id=(c - 1, t), device_id_type=MESH)

    @pl.when(has_next)
    def _():
        pl.semaphore_signal(barrier, inc=1, device_id=(c + 1, t), device_id_type=MESH)

    load_tok.start()
    load_dt.start()
    for k in range(K_PARTS):
        for copy in load(k):
            copy.start()
    load_out.start()

    peers = 2 + jnp.where(has_prev, 1, 0) + jnp.where(has_next, 1, 0)
    pl.semaphore_wait(barrier, peers)

    for k in range(K_PARTS):
        copy_a(k).start()
    for k in range(K_PARTS):
        copy_b(k).start()

    taps[:, 0:inner] = conv_x[...]
    taps[:, inner:wide] = conv_bc[...]
    acc[...] = jnp.zeros_like(acc)
    acc_dt[...] = jnp.zeros_like(acc_dt)

    @pl.when(c == 0)
    def _():
        ext[0:8, :] = jnp.zeros((8, wide), F32)
        st_in[...] = jnp.zeros_like(st_in)

    load_tok.wait()
    load_dt.wait()

    def project(k, _):
        ks = cols(k, kc)
        got(across, k, a_send, a_recv).wait_recv()
        copy_f(k).start()
        got(mate, k, b_send, b_recv).wait_recv()
        for copy in load(k):
            copy.wait()
        got(far, k, f_send, f_recv).wait_recv()
        lhs = gath[:, :, ks].reshape(span, kc)
        acc_dt[...] += dot(lhs, w_dt[ks, :])

        def tile(n, _):
            ns = cols(n, TILE)
            acc[:, ns] += dot(gath[:, :, ks].reshape(span, kc), w_in[ks, ns])
            return 0

        lax.fori_loop(0, wide // TILE, tile, 0)
        return 0

    lax.fori_loop(0, K_PARTS, project, 0)

    for n in range(wide // TILE):
        ns = slice(n * TILE, (n + 1) * TILE)
        ext[8 : 8 + span, ns] = acc[:, ns].astype(BF16).astype(F32)

    conv_send = remote(
        ext.at[span : span + 8, :], ext.at[0:8, :], conv_sem.at[0], conv_sem.at[1], c + 1, t
    )
    conv_recv = remote(
        ext.at[span : span + 8, :], ext.at[0:8, :], conv_sem.at[0], conv_sem.at[1], c - 1, t
    )

    @pl.when(has_next)
    def _():
        conv_send.start()

    dt = jax.nn.softplus(acc_dt[...] + dt_bias[...])
    la = -jnp.exp(a_log[...]) * dt
    later = lax.broadcasted_iota(jnp.int32, (span, span), 0)
    earlier = lax.broadcasted_iota(jnp.int32, (span, span), 1)
    tri = later >= earlier
    tri_b = jnp.where(tri, 1.0, 0.0).astype(BF16)
    cs = sum(dot(tri_b, term) for term in split(la, 3))
    cs_t = cs.T
    last = cs[span - 1 : span, :]
    head_width = inner // heads
    head_of = lax.broadcasted_iota(jnp.int32, (heads, inner), 1) // head_width
    head_at = lax.broadcasted_iota(jnp.int32, (heads, inner), 0)
    spread = jnp.where(head_of == head_at, 1.0, 0.0).astype(BF16)

    def expand(v):
        hi, lo = split(v, 2)
        return dot(hi, spread) + dot(lo, spread)

    ecs[...] = expand(jnp.exp(cs))
    skip = expand(jnp.broadcast_to(skip_d[...], (8, heads)))[0:1, :]
    dt_wide = expand(dt)
    dtail_wide = expand(dt * jnp.exp(last - cs))

    @pl.when(has_prev)
    def _():
        conv_recv.wait_recv()

    for n in range(wide // TILE):
        ns = slice(n * TILE, (n + 1) * TILE)
        total = taps[0:1, ns] * ext[5 : 5 + span, ns]
        for k in range(1, 4):
            total = total + taps[k : k + 1, ns] * ext[5 + k : 5 + k + span, ns]
        x = total / (1.0 + jnp.exp(-total))
        xc[:, ns] = x
        if n * TILE < inner:
            xdt[:, ns] = (x * dt_wide[:, ns]).astype(BF16)
            xtail[:, ns] = (x * dtail_wide[:, ns]).astype(BF16)

    b_t = xc[:, inner : inner + states].T.astype(BF16)
    c_b = xc[:, inner + states : wide].astype(BF16)
    end[...] = dot(b_t, xtail[...])

    parts = inner // LANES

    def state_send(j):
        return remote(st_out.at[j], st_in.at[j], s_send.at[j], s_recv.at[j], c + 1, t)

    def state_recv(j):
        return remote(st_out.at[j], st_in.at[j], s_send.at[j], s_recv.at[j], c - 1, t)

    def relay():
        for j in range(parts):
            ls = slice(j * LANES, (j + 1) * LANES)

            @pl.when(has_prev)
            def _():
                state_recv(j).wait_recv()

            @pl.when(has_next)
            def _():
                decay = ecs[span - 1 : span, ls]
                st_out[j] = (decay * st_in[j].astype(F32) + end[:, ls]).astype(BF16)
                state_send(j).start()

    @pl.when(c < 2)
    def _():
        relay()

    score[...] = jnp.where(tri, dot(c_b, b_t), 0.0)
    low_head = lax.broadcasted_iota(jnp.int32, (LANES, LANES), 1) < head_width
    for j in range(parts):
        ls = slice(j * LANES, (j + 1) * LANES)
        for r in range(span // LANES):
            rs = slice(r * LANES, (r + 1) * LANES)
            upto = (r + 1) * LANES
            both = []
            for h in (2 * j, 2 * j + 1):
                diff = cs[rs, h : h + 1] - cs_t[h : h + 1, 0:upto]
                weights = score[rs, 0:upto] * jnp.exp(jnp.minimum(diff, 0.0))
                both.append(dot(weights.astype(BF16), xdt[0:upto, ls]))
            yb[rs, ls] = jnp.where(low_head, both[0], both[1]) + skip[:, ls] * xc[rs, ls]

    @pl.when(c >= 2)
    def _():
        relay()

    same = (
        lax.broadcasted_iota(jnp.int32, (2 * LANES, LANES), 0) % LANES // head_width
        == lax.broadcasted_iota(jnp.int32, (2 * LANES, LANES), 1) // head_width
    )
    same = jnp.where(same, 1.0 / head_width, 0.0).astype(BF16)
    for j in range(parts):
        ls = slice(j * LANES, (j + 1) * LANES)
        y = yb[:, ls] + ecs[:, ls] * dot(c_b, st_in[j])
        mean_sq = dot(jnp.concatenate(split(y * y, 2), axis=1), same)
        normed[:, ls] = (y * lax.rsqrt(mean_sq + 1e-5) * gain[:, ls]).astype(BF16)

    load_out.wait()

    def hop1(j):
        return remote(send1.at[j], recv1.at[j], r1_send.at[j], r1_recv.at[j], c, mate)

    def hop2(j):
        return remote(send2.at[j], recv2.at[j], r2_send.at[j], r2_recv.at[j], c, across)

    def multiply(j):
        prod = dot(normed[...], w_out[:, cols(j, oc)])
        part[...] = prod.reshape(4, rows, oc)
        send1[j, 0] = part[far].astype(BF16)
        send1[j, 1] = part[mate].astype(BF16)
        hop1(j).start()
        own[j, 0] = part[across]
        own[j, 1] = part[t]

    def pass_on(j):
        hop1(j).wait_recv()
        send2[j] = (own[j, 0] + recv1[j, 0].astype(F32)).astype(BF16)
        hop2(j).start()

    multiply(0)

    def step(j, _):
        multiply(j)
        pass_on(j - 1)
        return 0

    lax.fori_loop(1, OUT_PARTS, step, 0)
    pass_on(OUT_PARTS - 1)

    def finish(j, _):
        hop2(j).wait_recv()
        total = own[j, 1] + recv1[j, 1].astype(F32) + recv2[j].astype(F32)
        out[:, cols(j, oc)] = total.astype(BF16)
        return 0

    lax.fori_loop(0, OUT_PARTS, finish, 0)

    def drain_k(k, _):
        copy_a(k).wait_send()
        copy_b(k).wait_send()
        copy_f(k).wait_send()
        return 0

    lax.fori_loop(0, K_PARTS, drain_k, 0)

    def drain_o(j, _):
        hop1(j).wait_send()
        hop2(j).wait_send()
        return 0

    lax.fori_loop(0, OUT_PARTS, drain_o, 0)

    @pl.when(has_next)
    def _():
        conv_send.wait_send()
        for j in range(parts):
            state_send(j).wait_send()


def per_device(
    ctx_size, tokens, in_x, in_bc, in_dt, conv_x, conv_bc, dt_bias, a_log, skip_d, norm_gain, out_w
):
    rows, depth = tokens.shape
    span = 4 * rows
    inner = in_x.shape[1]
    wide = inner + in_bc.shape[1]
    states = in_bc.shape[1] // 2
    heads = a_log.shape[0]
    parts = inner // LANES
    oc = depth // OUT_PARTS
    dma = pltpu.SemaphoreType.DMA
    anywhere = pl.BlockSpec(memory_space=pl.ANY)
    local = pl.BlockSpec(memory_space=pltpu.VMEM)
    return pl.pallas_call(
        functools.partial(layer_kernel, ctx_size),
        out_shape=jax.ShapeDtypeStruct((rows, depth), BF16),
        in_specs=[anywhere] * 5 + [local] * 6,
        out_specs=local,
        scratch_shapes=[
            pltpu.VMEM((4, rows, depth), BF16),
            pltpu.VMEM((depth, wide), BF16),
            pltpu.VMEM((depth, heads), BF16),
            pltpu.VMEM((inner, depth), BF16),
            pltpu.VMEM((span, wide), F32),
            pltpu.VMEM((span, heads), F32),
            pltpu.VMEM((span + 8, wide), F32),
            pltpu.VMEM((4, wide), F32),
            pltpu.VMEM((span, wide), F32),
            pltpu.VMEM((span, inner), BF16),
            pltpu.VMEM((span, inner), BF16),
            pltpu.VMEM((span, inner), F32),
            pltpu.VMEM((span, inner), F32),
            pltpu.VMEM((span, span), F32),
            pltpu.VMEM((states, inner), F32),
            pltpu.VMEM((parts, states, LANES), BF16),
            pltpu.VMEM((parts, states, LANES), BF16),
            pltpu.VMEM((span, inner), BF16),
            pltpu.VMEM((4, rows, oc), F32),
            pltpu.VMEM((OUT_PARTS, 2, rows, oc), F32),
            pltpu.VMEM((OUT_PARTS, 2, rows, oc), BF16),
            pltpu.VMEM((OUT_PARTS, 2, rows, oc), BF16),
            pltpu.VMEM((OUT_PARTS, rows, oc), BF16),
            pltpu.VMEM((OUT_PARTS, rows, oc), BF16),
            dma((3, K_PARTS)),
            dma(()),
            dma((K_PARTS,)),
            dma((K_PARTS,)),
            dma((K_PARTS,)),
            dma((K_PARTS,)),
            dma((K_PARTS,)),
            dma((K_PARTS,)),
            dma((2,)),
            dma((parts,)),
            dma((parts,)),
            dma((OUT_PARTS,)),
            dma((OUT_PARTS,)),
            dma((OUT_PARTS,)),
            dma((OUT_PARTS,)),
        ],
        compiler_params=pltpu.CompilerParams(
            collective_id=0, has_side_effects=True, vmem_limit_bytes=56 * 2**20
        ),
    )(
        tokens,
        in_x,
        in_bc,
        in_dt,
        out_w,
        conv_x,
        conv_bc,
        dt_bias.reshape(1, heads),
        a_log.reshape(1, heads),
        skip_d.reshape(1, heads),
        norm_gain.reshape(1, inner),
    )


def solution(mesh):
    return jax.shard_map(
        functools.partial(per_device, mesh.shape["ctx"]),
        mesh=mesh,
        in_specs=(
            P(("ctx", "tp"), None),
            P(None, "tp"),
            P(),
            P(None, "tp"),
            P(None, "tp"),
            P(),
            P("tp"),
            P("tp"),
            P("tp"),
            P("tp"),
            P("tp", None),
        ),
        out_specs=P(("ctx", "tp"), None),
        check_vma=False,
    )
```

time: 218 us -> 69 us (0.32); the launches traced: 214 us -> 68.7 us
  waiting for transfers between devices: 143 us -> 0 us
  Pallas kernels: 0 us -> 64.6 us
  matrix products: 31.6 us -> 0 us
  between operations: 13.6 us -> 0.01 us
  starting transfers between devices: 11.8 us -> 0 us
  other arithmetic: 9.68 us -> 0 us
    ppermute x9 -> x0, waiting for transfers between devices: 79.9 us -> none  [passed_along(): return lax.ppermute(shard, axis, pairs)]
    pallas_call x0 -> x1, Pallas kernels: none -> 64.6 us  [per_device(): pl.pallas_call(functools.partial(layer_kernel, ctx_size), out_shape=jax.S...]
    reduce_scatter x1 -> x0, waiting for transfers between devices: 41.2 us -> none  [per_device(): lax.psum_scatter(jnp.dot(normed, out_w, preferred_element_type=jnp.float3...]
    dot_general x9 -> x0, matrix products: 31.6 us -> none  [the longest x1 7.09 us: per_device(): jnp.dot(normed, out_w, preferred_element_type=jnp.float32)]
    all_gather x1 -> x0, waiting for transfers between devices: 21.4 us -> none  [per_device(): gathered = lax.all_gather(tokens, 'tp', axis=0, tiled=True)]
    ppermute x9 -> x0, starting transfers between devices: 11.7 us -> none  [passed_along(): return lax.ppermute(shard, axis, pairs)]
    add x8 -> x0, other arithmetic: 7.04 us -> none  [the longest x7 6.36 us: relay(): outgoing = span_decay[:, None, None] * incoming + end_state]
    unnamed x8 -> x2, local copies, waits for them, and re-layouts: 0.02 us -> 4.11 us
  transfers between devices with their start and end apart: 11 -> 0, of which waited for: 10 -> 0; matrix products, arithmetic and copies ran while one was open for 5% -> 0% of each run, Pallas kernels for 0% -> 0%
where the time goes in v1:
time: 69 us; the launch traced here: 68.7 us
  Pallas kernels  64.6 us (94%)
  local copies, waits for them, and re-layouts  4.11 us (6%)
    pallas_call x1, Pallas kernels, per_device(): pl.pallas_call(functools.partial(layer_kernel, ctx_size), out_shape=jax.S...  64.6 us
    unnamed x2, local copies, waits for them, and re-layouts  4.11 us

profile of v1, /device:TPU:31, one launch (start us, length us, event | category | flops | bytes accessed | tf_op | source)
XLA Modules:
  0.0 68.7 jit_solution(13969950389830961569)
XLA Ops:
  0.0 2.2 %copy.12.in_dt = bf16[4096,16]{1,0:T(8,128)(2,1)} copy(bf16[4096,16]{0,1:T(8,128)(2,1)} %param.14) | data formatting | bytes 262144 | tf_op args[3]
  2.2 64.6 %shard_map.109 = bf16[64,4096]{1,0:T(8,128)(2,1)} custom-call(bf16[64,4096]{1,0:T(8,128)(2,1)} %tokens.1, bf16[4096,1024]{1,0:T(8,128)(2,1)} %in_x.1, bf16[4096,256]{1,0:T(8,128)(2,1)} %in_bc.1, bf16[4096,16]{1,0:T(8,128)(2,1)} %copy.12.in_dt, bf16[1024,4096]{1,0:T(8,128)(2,1)} %out_w.1, f32[4,1024]{1,0:T(4,128)} %conv_x.1, f32[4,256]{1,0:T(4,128)} %conv_bc.1, ...), custom_call_target="tpu_custom_call" | custom-call | tf_op jit(solution)/shard_map/pallas_call | solution.py:398
  66.9 1.9 %copy.14 = bf16[64,4096]{1,0:T(8,128)(2,1)} copy(bf16[64,4096]{1,0:T(8,128)(2,1)} %shard_map.109) | data formatting | bytes 1048576

commit v2 on v1

--- a/solution.py
+++ b/solution.py
@@ -10,7 +10,7 @@
 MESH = pl.DeviceIdType.MESH
 F32 = jnp.float32
 BF16 = jnp.bfloat16
-K_PARTS = 4
+K_PARTS = 8
 OUT_PARTS = 8
 TILE = 256
 LANES = 128
@@ -59,7 +59,12 @@
     score,
     end,
     st_in,
-    st_out,
+    x_out,
+    x_in,
+    g_out,
+    g_in,
+    p_out,
+    pair_decay,
     normed,
     part,
     own,
@@ -76,8 +81,13 @@
     f_send,
     f_recv,
     conv_sem,
-    s_send,
-    s_recv,
+    d_sem,
+    x_send,
+    x_recv,
+    g_send,
+    g_recv,
+    p_send,
+    p_recv,
     r1_send,
     r1_recv,
     r2_send,
@@ -99,6 +109,12 @@
     oc = depth // OUT_PARTS
     has_prev = c > 0
     has_next = c < ctx_size - 1
+    has_prev2 = c > 1
+    has_next2 = c < ctx_size - 2
+    odd = c % 2
+    pair = c + 1 - 2 * odd
+    parts = inner // LANES
+    half = parts // 2
 
     def cols(i, size):
         return pl.ds(pl.multiple_of(i * size, size), size)
@@ -158,6 +174,14 @@
     def _():
         pl.semaphore_signal(barrier, inc=1, device_id=(c + 1, t), device_id_type=MESH)
 
+    @pl.when(has_prev2)
+    def _():
+        pl.semaphore_signal(barrier, inc=1, device_id=(c - 2, t), device_id_type=MESH)
+
+    @pl.when(has_next2)
+    def _():
+        pl.semaphore_signal(barrier, inc=1, device_id=(c + 2, t), device_id_type=MESH)
+
     load_tok.start()
     load_dt.start()
     for k in range(K_PARTS):
@@ -165,7 +189,9 @@
             copy.start()
     load_out.start()
 
-    peers = 2 + jnp.where(has_prev, 1, 0) + jnp.where(has_next, 1, 0)
+    peers = 2
+    for flag in (has_prev, has_next, has_prev2, has_next2):
+        peers = peers + jnp.where(flag, 1, 0)
     pl.semaphore_wait(barrier, peers)
 
     for k in range(K_PARTS):
@@ -181,7 +207,10 @@
     @pl.when(c == 0)
     def _():
         ext[0:8, :] = jnp.zeros((8, wide), F32)
-        st_in[...] = jnp.zeros_like(st_in)
+
+    @pl.when(c < 2)
+    def _():
+        g_in[...] = jnp.zeros_like(g_in)
 
     load_tok.wait()
     load_dt.wait()
@@ -195,7 +224,9 @@
             copy.wait()
         got(far, k, f_send, f_recv).wait_recv()
         lhs = gath[:, :, ks].reshape(span, kc)
-        acc_dt[...] += dot(lhs, w_dt[ks, :])
+        acc_dt[...] += lax.dot_general(
+            lhs, w_dt[:, ks], (((1,), (1,)), ((), ())), preferred_element_type=F32
+        )
 
         def tile(n, _):
             ns = cols(n, TILE)
@@ -207,10 +238,7 @@
 
     lax.fori_loop(0, K_PARTS, project, 0)
 
-    for n in range(wide // TILE):
-        ns = slice(n * TILE, (n + 1) * TILE)
-        ext[8 : 8 + span, ns] = acc[:, ns].astype(BF16).astype(F32)
-
+    ext[span : span + 8, :] = acc[span - 8 : span, :].astype(BF16).astype(F32)
     conv_send = remote(
         ext.at[span : span + 8, :], ext.at[0:8, :], conv_sem.at[0], conv_sem.at[1], c + 1, t
     )
@@ -221,6 +249,10 @@
     @pl.when(has_next)
     def _():
         conv_send.start()
+
+    for n in range(wide // TILE):
+        ns = slice(n * TILE, (n + 1) * TILE)
+        ext[8:span, ns] = acc[0 : span - 8, ns].astype(BF16).astype(F32)
 
     dt = jax.nn.softplus(acc_dt[...] + dt_bias[...])
     la = -jnp.exp(a_log[...]) * dt
@@ -241,6 +273,12 @@
         return dot(hi, spread) + dot(lo, spread)
 
     ecs[...] = expand(jnp.exp(cs))
+
+    theirs = cols(1 - odd, inner // 2)
+    decay_swap = remote(
+        ecs.at[span - 8 : span, theirs], pair_decay, d_sem.at[0], d_sem.at[1], pair, t
+    )
+    decay_swap.start()
     skip = expand(jnp.broadcast_to(skip_d[...], (8, heads)))[0:1, :]
     dt_wide = expand(dt)
     dtail_wide = expand(dt * jnp.exp(last - cs))
@@ -262,29 +300,66 @@
 
     b_t = xc[:, inner : inner + states].T.astype(BF16)
     c_b = xc[:, inner + states : wide].astype(BF16)
-    end[...] = dot(b_t, xtail[...])
-
-    parts = inner // LANES
-
-    def state_send(j):
-        return remote(st_out.at[j], st_in.at[j], s_send.at[j], s_recv.at[j], c + 1, t)
-
-    def state_recv(j):
-        return remote(st_out.at[j], st_in.at[j], s_send.at[j], s_recv.at[j], c - 1, t)
+
+    def end_swap(i):
+        return remote(x_out.at[i], x_in.at[i], x_send.at[i], x_recv.at[i], pair, t)
+
+    def hand_down(i, cc):
+        return remote(g_out.at[i], g_in.at[i], g_send.at[i], g_recv.at[i], cc, t)
+
+    def share(i):
+        j = odd * half + i
+        return remote(p_out.at[i], st_in.at[j], p_send.at[i], p_recv.at[i], pair, t)
+
+    def shared(i):
+        j = (1 - odd) * half + i
+        return remote(p_out.at[i], st_in.at[j], p_send.at[i], p_recv.at[i], pair, t)
+
+    def ends(i, _):
+        j = (1 - odd) * half + i
+        x_out[i] = dot(b_t, xtail[:, cols(j, LANES)]).astype(BF16)
+        end_swap(i).start()
+        return 0
+
+    def own_ends(i, _):
+        j = odd * half + i
+        end[i] = dot(b_t, xtail[:, cols(j, LANES)])
+        return 0
+
+    lax.fori_loop(0, half, ends, 0)
+    lax.fori_loop(0, half, own_ends, 0)
+    decay_swap.wait_recv()
 
     def relay():
-        for j in range(parts):
-            ls = slice(j * LANES, (j + 1) * LANES)
-
-            @pl.when(has_prev)
+        def part_of(i, _):
+            ls = cols(i, LANES)
+            mine = ecs[span - 8 : span, cols(odd * half + i, LANES)][7:8, :]
+            other = pair_decay[:, ls][7:8, :]
+            end_swap(i).wait_recv()
+            end_mine = end[i]
+            end_other = x_in[i].astype(F32)
+
+            @pl.when(has_prev2)
             def _():
-                state_recv(j).wait_recv()
-
-            @pl.when(has_next)
+                hand_down(i, c - 2).wait_recv()
+
+            even = odd == 0
+            first = g_in[i].astype(F32)
+            second = jnp.where(even, mine, other) * first + jnp.where(even, end_mine, end_other)
+
+            @pl.when(has_next2)
             def _():
-                decay = ecs[span - 1 : span, ls]
-                st_out[j] = (decay * st_in[j].astype(F32) + end[:, ls]).astype(BF16)
-                state_send(j).start()
+                after = jnp.where(even, other, mine) * second
+                after = after + jnp.where(even, end_other, end_mine)
+                g_out[i] = after.astype(BF16)
+                hand_down(i, c + 2).start()
+
+            p_out[i] = jnp.where(even, second, first).astype(BF16)
+            share(i).start()
+            st_in[odd * half + i] = jnp.where(even, first, second).astype(BF16)
+            return 0
+
+        lax.fori_loop(0, half, part_of, 0)
 
     @pl.when(c < 2)
     def _():
@@ -293,6 +368,12 @@
     score[...] = jnp.where(tri, dot(c_b, b_t), 0.0)
     low_head = lax.broadcasted_iota(jnp.int32, (LANES, LANES), 1) < head_width
     for j in range(parts):
+        if j == parts // 2:
+
+            @pl.when((c >= 2) & (c < 4))
+            def _():
+                relay()
+
         ls = slice(j * LANES, (j + 1) * LANES)
         for r in range(span // LANES):
             rs = slice(r * LANES, (r + 1) * LANES)
@@ -304,7 +385,7 @@
                 both.append(dot(weights.astype(BF16), xdt[0:upto, ls]))
             yb[rs, ls] = jnp.where(low_head, both[0], both[1]) + skip[:, ls] * xc[rs, ls]
 
-    @pl.when(c >= 2)
+    @pl.when(c >= 4)
     def _():
         relay()
 
@@ -313,6 +394,8 @@
         == lax.broadcasted_iota(jnp.int32, (2 * LANES, LANES), 1) // head_width
     )
     same = jnp.where(same, 1.0 / head_width, 0.0).astype(BF16)
+    for i in range(half):
+        shared(i).wait_recv()
     for j in range(parts):
         ls = slice(j * LANES, (j + 1) * LANES)
         y = yb[:, ls] + ecs[:, ls] * dot(c_b, st_in[j])
@@ -354,7 +437,7 @@
     def finish(j, _):
         hop2(j).wait_recv()
         total = own[j, 1] + recv1[j, 1].astype(F32) + recv2[j].astype(F32)
-        out[:, cols(j, oc)] = total.astype(BF16)
+        out[:, cols(j, oc)] = total
         return 0
 
     lax.fori_loop(0, OUT_PARTS, finish, 0)
@@ -374,11 +457,26 @@
 
     lax.fori_loop(0, OUT_PARTS, drain_o, 0)
 
+    decay_swap.wait_send()
+
+    def drain_s(i, _):
+        end_swap(i).wait_send()
+        share(i).wait_send()
+        return 0
+
+    lax.fori_loop(0, half, drain_s, 0)
+
     @pl.when(has_next)
     def _():
         conv_send.wait_send()
-        for j in range(parts):
-            state_send(j).wait_send()
+
+    @pl.when(has_next2)
+    def _():
+        def drain_g(i, _):
+            hand_down(i, c + 2).wait_send()
+            return 0
+
+        lax.fori_loop(0, half, drain_g, 0)
 
 
 def per_device(
@@ -391,19 +489,20 @@
     states = in_bc.shape[1] // 2
     heads = a_log.shape[0]
     parts = inner // LANES
+    half = parts // 2
     oc = depth // OUT_PARTS
     dma = pltpu.SemaphoreType.DMA
     anywhere = pl.BlockSpec(memory_space=pl.ANY)
     local = pl.BlockSpec(memory_space=pltpu.VMEM)
-    return pl.pallas_call(
+    total = pl.pallas_call(
         functools.partial(layer_kernel, ctx_size),
-        out_shape=jax.ShapeDtypeStruct((rows, depth), BF16),
+        out_shape=jax.ShapeDtypeStruct((rows, depth), F32),
         in_specs=[anywhere] * 5 + [local] * 6,
         out_specs=local,
         scratch_shapes=[
             pltpu.VMEM((4, rows, depth), BF16),
             pltpu.VMEM((depth, wide), BF16),
-            pltpu.VMEM((depth, heads), BF16),
+            pltpu.VMEM((heads, depth), BF16),
             pltpu.VMEM((inner, depth), BF16),
             pltpu.VMEM((span, wide), F32),
             pltpu.VMEM((span, heads), F32),
@@ -415,9 +514,14 @@
             pltpu.VMEM((span, inner), F32),
             pltpu.VMEM((span, inner), F32),
             pltpu.VMEM((span, span), F32),
-            pltpu.VMEM((states, inner), F32),
+            pltpu.VMEM((half, states, LANES), F32),
             pltpu.VMEM((parts, states, LANES), BF16),
-            pltpu.VMEM((parts, states, LANES), BF16),
+            pltpu.VMEM((half, states, LANES), BF16),
+            pltpu.VMEM((half, states, LANES), BF16),
+            pltpu.VMEM((half, states, LANES), BF16),
+            pltpu.VMEM((half, states, LANES), BF16),
+            pltpu.VMEM((half, states, LANES), BF16),
+            pltpu.VMEM((8, inner // 2), F32),
             pltpu.VMEM((span, inner), BF16),
             pltpu.VMEM((4, rows, oc), F32),
             pltpu.VMEM((OUT_PARTS, 2, rows, oc), F32),
@@ -434,8 +538,13 @@
             dma((K_PARTS,)),
             dma((K_PARTS,)),
             dma((2,)),
-            dma((parts,)),
-            dma((parts,)),
+            dma((2,)),
+            dma((half,)),
+            dma((half,)),
+            dma((half,)),
+            dma((half,)),
+            dma((half,)),
+            dma((half,)),
             dma((OUT_PARTS,)),
             dma((OUT_PARTS,)),
             dma((OUT_PARTS,)),
@@ -448,7 +557,7 @@
         tokens,
         in_x,
         in_bc,
-        in_dt,
+        in_dt.T,
         out_w,
         conv_x,
         conv_bc,
@@ -457,6 +566,7 @@
         skip_d.reshape(1, heads),
         norm_gain.reshape(1, inner),
     )
+    return total.astype(BF16)
 
 
 def solution(mesh):

time: 69 us -> 65.1 us (0.943)
  local copies, waits for them, and re-layouts: 4.11 us -> 0 us
  other arithmetic: 0 us -> 2.07 us
  Pallas kernels: 64.6 us -> 62.8 us
    unnamed x2 -> x0, local copies, waits for them, and re-layouts: 4.11 us -> none
    convert_element_type x0 -> x1, other arithmetic: none -> 2.07 us  [per_device(): return total.astype(BF16)]
    pallas_call x1, Pallas kernels: 64.6 us -> 62.8 us  [per_device(): pl.pallas_call(functools.partial(layer_kernel, ctx_size), out_shape=jax.S...]
where the time goes in v2:
time: 65.1 us; the launch traced here: 64.9 us
  Pallas kernels  62.8 us (96%)
  other arithmetic  2.07 us (3%)
    pallas_call x1, Pallas kernels, per_device(): pl.pallas_call(functools.partial(layer_kernel, ctx_size), out_shape=jax.S...  62.8 us
    convert_element_type x1, other arithmetic, per_device(): return total.astype(BF16)  2.07 us

profile of v2, /device:TPU:31, one launch (start us, length us, event | category | flops | bytes accessed | tf_op | source)
XLA Modules:
  0.0 64.9 jit_solution(15063109675678671262)
XLA Ops:
  0.0 62.8 %shard_map.109 = f32[64,4096]{1,0:T(8,128)} custom-call(bf16[64,4096]{1,0:T(8,128)(2,1)} %tokens.1, bf16[4096,1024]{1,0:T(8,128)(2,1)} %in_x.1, bf16[4096,256]{1,0:T(8,128)(2,1)} %in_bc.1, bf16[16,4096]{1,0:T(8,128)(2,1)} %bitcast.5, bf16[1024,4096]{1,0:T(8,128)(2,1)} %out_w.1, f32[4,1024]{1,0:T(4,128)} %conv_x.1, f32[4,256]{1,0:T(4,128)} %conv_bc.1, ...), custom_call_target="tpu_custom_call" | custom-call | tf_op jit(solution)/shard_map/pallas_call | solution.py:497
  62.8 2.1 %convert_element_type.3 = bf16[64,4096]{1,0:T(8,128)(2,1)} convert(f32[64,4096]{1,0:T(8,128)} %shard_map.109) | non-fusion elementwise | flops 262144 | bytes 1572864 | tf_op jit(solution)/shard_map/convert_element_type | solution.py:569

commit v3 on v2

--- a/solution.py
+++ b/solution.py
@@ -55,6 +55,8 @@
     xdt,
     xtail,
     ecs,
+    tri_t,
+    spread,
     yb,
     score,
     end,
@@ -212,6 +214,28 @@
     def _():
         g_in[...] = jnp.zeros_like(g_in)
 
+    head_width = inner // heads
+    fields = 8 * heads
+    earlier = lax.broadcasted_iota(jnp.int32, (span, span), 0)
+    later = lax.broadcasted_iota(jnp.int32, (span, span), 1)
+    tri_t[...] = jnp.where(later >= earlier, 1.0, 0.0).astype(BF16)
+    field = lax.broadcasted_iota(jnp.int32, (fields, 3 * LANES), 0)
+    lane = lax.broadcasted_iota(jnp.int32, (fields, 3 * LANES), 1)
+    for j in range(parts):
+        head = (lane % LANES + j * LANES) // head_width
+        hit = (field % heads == head) & (field // (2 * heads) == lane // LANES)
+        spread[j] = jnp.where(hit, 1.0, 0.0).astype(BF16)
+    eye = lax.broadcasted_iota(jnp.int32, (heads, heads), 0) == lax.broadcasted_iota(
+        jnp.int32, (heads, heads), 1
+    )
+
+    def upright(row):
+        return jnp.sum(jnp.where(eye, row, 0.0), axis=1, keepdims=True)
+
+    bias = upright(dt_bias[...])
+    rate = -jnp.exp(upright(a_log[...]))
+    skip_col = jnp.broadcast_to(upright(skip_d[...]), (heads, LANES))
+
     load_tok.wait()
     load_dt.wait()
 
@@ -225,15 +249,12 @@
         got(far, k, f_send, f_recv).wait_recv()
         lhs = gath[:, :, ks].reshape(span, kc)
         acc_dt[...] += lax.dot_general(
-            lhs, w_dt[:, ks], (((1,), (1,)), ((), ())), preferred_element_type=F32
+            w_dt[:, ks], lhs, (((1,), (1,)), ((), ())), preferred_element_type=F32
         )
 
-        def tile(n, _):
-            ns = cols(n, TILE)
-            acc[:, ns] += dot(gath[:, :, ks].reshape(span, kc), w_in[ks, ns])
-            return 0
-
-        lax.fori_loop(0, wide // TILE, tile, 0)
+        for n in range(wide // TILE):
+            ns = slice(n * TILE, (n + 1) * TILE)
+            acc[:, ns] += dot(lhs, w_in[ks, ns])
         return 0
 
     lax.fori_loop(0, K_PARTS, project, 0)
@@ -254,49 +275,50 @@
         ns = slice(n * TILE, (n + 1) * TILE)
         ext[8:span, ns] = acc[0 : span - 8, ns].astype(BF16).astype(F32)
 
-    dt = jax.nn.softplus(acc_dt[...] + dt_bias[...])
-    la = -jnp.exp(a_log[...]) * dt
-    later = lax.broadcasted_iota(jnp.int32, (span, span), 0)
-    earlier = lax.broadcasted_iota(jnp.int32, (span, span), 1)
-    tri = later >= earlier
-    tri_b = jnp.where(tri, 1.0, 0.0).astype(BF16)
-    cs = sum(dot(tri_b, term) for term in split(la, 3))
-    cs_t = cs.T
-    last = cs[span - 1 : span, :]
-    head_width = inner // heads
-    head_of = lax.broadcasted_iota(jnp.int32, (heads, inner), 1) // head_width
-    head_at = lax.broadcasted_iota(jnp.int32, (heads, inner), 0)
-    spread = jnp.where(head_of == head_at, 1.0, 0.0).astype(BF16)
-
-    def expand(v):
-        hi, lo = split(v, 2)
-        return dot(hi, spread) + dot(lo, spread)
-
-    ecs[...] = expand(jnp.exp(cs))
+    v = acc_dt[...] + bias
+    dt = jnp.maximum(v, 0.0) + jnp.log1p(jnp.exp(-jnp.abs(v)))
+    sums = dot(jnp.concatenate(split(rate * dt, 3), axis=0), tri_t[...])
+    cs_t = sums[0:heads] + sums[heads : 2 * heads] + sums[2 * heads :]
+    tail = jnp.exp(cs_t[:, span - 1 : span] - cs_t)
+    rows_of = []
+    for quantity in (dt, dt * tail, jnp.exp(cs_t)):
+        rows_of += [term.astype(F32) for term in split(quantity, 2)]
+    cs_wide = jnp.concatenate(rows_of + [cs_t, jnp.zeros_like(cs_t)], axis=0).T
+    cs = cs_wide[:, 6 * heads : 7 * heads]
+    wide_b = cs_wide.astype(BF16)
+    for j in range(parts):
+        ls = slice(j * LANES, (j + 1) * LANES)
+        ecs[span - 8 : span, ls] = dot(wide_b[span - 16 : span], spread[j])[8:16, 2 * LANES :]
 
     theirs = cols(1 - odd, inner // 2)
     decay_swap = remote(
         ecs.at[span - 8 : span, theirs], pair_decay, d_sem.at[0], d_sem.at[1], pair, t
     )
     decay_swap.start()
-    skip = expand(jnp.broadcast_to(skip_d[...], (8, heads)))[0:1, :]
-    dt_wide = expand(dt)
-    dtail_wide = expand(dt * jnp.exp(last - cs))
 
     @pl.when(has_prev)
     def _():
         conv_recv.wait_recv()
 
-    for n in range(wide // TILE):
-        ns = slice(n * TILE, (n + 1) * TILE)
-        total = taps[0:1, ns] * ext[5 : 5 + span, ns]
-        for k in range(1, 4):
-            total = total + taps[k : k + 1, ns] * ext[5 + k : 5 + k + span, ns]
-        x = total / (1.0 + jnp.exp(-total))
-        xc[:, ns] = x
-        if n * TILE < inner:
-            xdt[:, ns] = (x * dt_wide[:, ns]).astype(BF16)
-            xtail[:, ns] = (x * dtail_wide[:, ns]).astype(BF16)
+    step_rows = 64
+    for n in list(range(inner // LANES, wide // LANES)) + list(range(parts)):
+        ns = slice(n * LANES, (n + 1) * LANES)
+        if n < parts:
+            scales = dot(wide_b, spread[n])
+        for r in range(0, span, step_rows):
+            rs = slice(r, r + step_rows)
+            total = taps[0:1, ns] * ext[5 + r : 5 + r + step_rows, ns]
+            for k in range(1, 4):
+                total = total + taps[k : k + 1, ns] * ext[5 + k + r : 5 + k + r + step_rows, ns]
+            x = total / (1.0 + jnp.exp(-total))
+            xc[rs, ns] = x
+            if n < parts:
+                xdt[rs, ns] = (x * scales[rs, 0:LANES]).astype(BF16)
+                xtail[rs, ns] = (x * scales[rs, LANES : 2 * LANES]).astype(BF16)
+                if r + step_rows < span:
+                    ecs[rs, ns] = scales[rs, 2 * LANES :]
+                else:
+                    ecs[r : span - 8, ns] = scales[r : span - 8, 2 * LANES :]
 
     b_t = xc[:, inner : inner + states].T.astype(BF16)
     c_b = xc[:, inner + states : wide].astype(BF16)
@@ -315,19 +337,16 @@
         j = (1 - odd) * half + i
         return remote(p_out.at[i], st_in.at[j], p_send.at[i], p_recv.at[i], pair, t)
 
-    def ends(i, _):
-        j = (1 - odd) * half + i
-        x_out[i] = dot(b_t, xtail[:, cols(j, LANES)]).astype(BF16)
+    theirs_end = dot(b_t, xtail[:, theirs]).astype(BF16)
+    for i in range(half):
+        x_out[i] = theirs_end[:, i * LANES : (i + 1) * LANES]
         end_swap(i).start()
-        return 0
-
-    def own_ends(i, _):
-        j = odd * half + i
-        end[i] = dot(b_t, xtail[:, cols(j, LANES)])
-        return 0
-
-    lax.fori_loop(0, half, ends, 0)
-    lax.fori_loop(0, half, own_ends, 0)
+    mine_end = dot(b_t, xtail[:, cols(odd, inner // 2)])
+    for i in range(half):
+        end[i] = mine_end[:, i * LANES : (i + 1) * LANES]
+    later = lax.broadcasted_iota(jnp.int32, (span, span), 0)
+    earlier = lax.broadcasted_iota(jnp.int32, (span, span), 1)
+    score[...] = jnp.where(later >= earlier, dot(c_b, b_t), 0.0)
     decay_swap.wait_recv()
 
     def relay():
@@ -365,7 +384,7 @@
     def _():
         relay()
 
-    score[...] = jnp.where(tri, dot(c_b, b_t), 0.0)
+    low_row = lax.broadcasted_iota(jnp.int32, (1, LANES), 1) < head_width
     low_head = lax.broadcasted_iota(jnp.int32, (LANES, LANES), 1) < head_width
     for j in range(parts):
         if j == parts // 2:
@@ -383,7 +402,8 @@
                 diff = cs[rs, h : h + 1] - cs_t[h : h + 1, 0:upto]
                 weights = score[rs, 0:upto] * jnp.exp(jnp.minimum(diff, 0.0))
                 both.append(dot(weights.astype(BF16), xdt[0:upto, ls]))
-            yb[rs, ls] = jnp.where(low_head, both[0], both[1]) + skip[:, ls] * xc[rs, ls]
+            skip = jnp.where(low_row, skip_col[2 * j : 2 * j + 1], skip_col[2 * j + 1 : 2 * j + 2])
+            yb[rs, ls] = jnp.where(low_head, both[0], both[1]) + skip * xc[rs, ls]
 
     @pl.when(c >= 4)
     def _():
@@ -394,13 +414,18 @@
         == lax.broadcasted_iota(jnp.int32, (2 * LANES, LANES), 1) // head_width
     )
     same = jnp.where(same, 1.0 / head_width, 0.0).astype(BF16)
-    for i in range(half):
-        shared(i).wait_recv()
-    for j in range(parts):
-        ls = slice(j * LANES, (j + 1) * LANES)
+
+    def finish_heads(j):
+        ls = cols(j, LANES)
         y = yb[:, ls] + ecs[:, ls] * dot(c_b, st_in[j])
         mean_sq = dot(jnp.concatenate(split(y * y, 2), axis=1), same)
         normed[:, ls] = (y * lax.rsqrt(mean_sq + 1e-5) * gain[:, ls]).astype(BF16)
+
+    for i in range(half):
+        finish_heads(odd * half + i)
+    for i in range(half):
+        shared(i).wait_recv()
+        finish_heads((1 - odd) * half + i)
 
     load_out.wait()
 
@@ -437,7 +462,7 @@
     def finish(j, _):
         hop2(j).wait_recv()
         total = own[j, 1] + recv1[j, 1].astype(F32) + recv2[j].astype(F32)
-        out[:, cols(j, oc)] = total
+        out[:, cols(j, oc)] = total.astype(BF16)
         return 0
 
     lax.fori_loop(0, OUT_PARTS, finish, 0)
@@ -494,9 +519,9 @@
     dma = pltpu.SemaphoreType.DMA
     anywhere = pl.BlockSpec(memory_space=pl.ANY)
     local = pl.BlockSpec(memory_space=pltpu.VMEM)
-    total = pl.pallas_call(
+    return pl.pallas_call(
         functools.partial(layer_kernel, ctx_size),
-        out_shape=jax.ShapeDtypeStruct((rows, depth), F32),
+        out_shape=jax.ShapeDtypeStruct((rows, depth), BF16),
         in_specs=[anywhere] * 5 + [local] * 6,
         out_specs=local,
         scratch_shapes=[
@@ -505,13 +530,15 @@
             pltpu.VMEM((heads, depth), BF16),
             pltpu.VMEM((inner, depth), BF16),
             pltpu.VMEM((span, wide), F32),
-            pltpu.VMEM((span, heads), F32),
+            pltpu.VMEM((heads, span), F32),
             pltpu.VMEM((span + 8, wide), F32),
             pltpu.VMEM((4, wide), F32),
             pltpu.VMEM((span, wide), F32),
             pltpu.VMEM((span, inner), BF16),
             pltpu.VMEM((span, inner), BF16),
             pltpu.VMEM((span, inner), F32),
+            pltpu.VMEM((span, span), BF16),
+            pltpu.VMEM((parts, 8 * heads, 3 * LANES), BF16),
             pltpu.VMEM((span, inner), F32),
             pltpu.VMEM((span, span), F32),
             pltpu.VMEM((half, states, LANES), F32),
@@ -566,7 +593,6 @@
         skip_d.reshape(1, heads),
         norm_gain.reshape(1, inner),
     )
-    return total.astype(BF16)
 
 
 def solution(mesh):

time: 65.1 us -> 58.5 us (0.90)
  Pallas kernels: 62.8 us -> 56.4 us
  other arithmetic: 2.07 us -> 0 us
  local copies, waits for them, and re-layouts: 0 us -> 1.87 us
    pallas_call x1, Pallas kernels: 62.8 us -> 56.4 us  [per_device(): pl.pallas_call(functools.partial(layer_kernel, ctx_size), out_shape=jax.S...]
    convert_element_type x1 -> x0, other arithmetic: 2.07 us -> none  [per_device(): return total.astype(BF16)]
    unnamed x0 -> x1, local copies, waits for them, and re-layouts: none -> 1.87 us
where the time goes in v3:
time: 58.5 us; the launch traced here: 58.3 us
  Pallas kernels  56.4 us (96%)
  local copies, waits for them, and re-layouts  1.87 us (3%)
    pallas_call x1, Pallas kernels, per_device(): pl.pallas_call(functools.partial(layer_kernel, ctx_size), out_shape=jax.S...  56.4 us
    unnamed x1, local copies, waits for them, and re-layouts  1.87 us

profile of v3, /device:TPU:31, one launch (start us, length us, event | category | flops | bytes accessed | tf_op | source)
XLA Modules:
  0.0 58.3 jit_solution(2379888317611785961)
XLA Ops:
  0.0 56.4 %shard_map.109 = bf16[64,4096]{1,0:T(8,128)(2,1)} custom-call(bf16[64,4096]{1,0:T(8,128)(2,1)} %tokens.1, bf16[4096,1024]{1,0:T(8,128)(2,1)} %in_x.1, bf16[4096,256]{1,0:T(8,128)(2,1)} %in_bc.1, bf16[16,4096]{1,0:T(8,128)(2,1)} %bitcast.5, bf16[1024,4096]{1,0:T(8,128)(2,1)} %out_w.1, f32[4,1024]{1,0:T(4,128)} %conv_x.1, f32[4,256]{1,0:T(4,128)} %conv_bc.1, ...), custom_call_target="tpu_custom_call" | custom-call | tf_op jit(solution)/shard_map/pallas_call | solution.py:522
  56.4 1.9 %copy.13 = bf16[64,4096]{1,0:T(8,128)(2,1)} copy(bf16[64,4096]{1,0:T(8,128)(2,1)} %shard_map.109) | data formatting | bytes 1048576

commit v4 on v3

--- a/solution.py
+++ b/solution.py
@@ -11,7 +11,7 @@
 F32 = jnp.float32
 BF16 = jnp.bfloat16
 K_PARTS = 8
-OUT_PARTS = 8
+OUT_PARTS = 16
 TILE = 256
 LANES = 128
 
@@ -189,7 +189,6 @@
     for k in range(K_PARTS):
         for copy in load(k):
             copy.start()
-    load_out.start()
 
     peers = 2
     for flag in (has_prev, has_next, has_prev2, has_next2):
@@ -258,6 +257,7 @@
         return 0
 
     lax.fori_loop(0, K_PARTS, project, 0)
+    load_out.start()
 
     ext[span : span + 8, :] = acc[span - 8 : span, :].astype(BF16).astype(F32)
     conv_send = remote(
@@ -296,29 +296,41 @@
     )
     decay_swap.start()
 
+    step_rows = 64
+
+    def conv(ns, r, scales):
+        rs = slice(r, r + step_rows)
+        total = taps[0:1, ns] * ext[5 + r : 5 + r + step_rows, ns]
+        for k in range(1, 4):
+            total = total + taps[k : k + 1, ns] * ext[5 + k + r : 5 + k + r + step_rows, ns]
+        x = total / (1.0 + jnp.exp(-total))
+        xc[rs, ns] = x
+        if scales is not None:
+            xdt[rs, ns] = (x * scales[rs, 0:LANES]).astype(BF16)
+            xtail[rs, ns] = (x * scales[rs, LANES : 2 * LANES]).astype(BF16)
+            upto = min(r + step_rows, span - 8)
+            ecs[r:upto, ns] = scales[r:upto, 2 * LANES :]
+
+    bc_tiles = [slice(n, n + LANES) for n in range(inner, wide, LANES)]
+    for ns in bc_tiles:
+        for r in range(step_rows, span, step_rows):
+            conv(ns, r, None)
+    tiles = []
+    for i in range(half):
+        n = (1 - odd) * half + i
+        scales = dot(wide_b, spread[n])
+        tiles.append((cols(n, LANES), scales))
+        for r in range(step_rows, span, step_rows):
+            conv(cols(n, LANES), r, scales)
+
     @pl.when(has_prev)
     def _():
         conv_recv.wait_recv()
 
-    step_rows = 64
-    for n in list(range(inner // LANES, wide // LANES)) + list(range(parts)):
-        ns = slice(n * LANES, (n + 1) * LANES)
-        if n < parts:
-            scales = dot(wide_b, spread[n])
-        for r in range(0, span, step_rows):
-            rs = slice(r, r + step_rows)
-            total = taps[0:1, ns] * ext[5 + r : 5 + r + step_rows, ns]
-            for k in range(1, 4):
-                total = total + taps[k : k + 1, ns] * ext[5 + k + r : 5 + k + r + step_rows, ns]
-            x = total / (1.0 + jnp.exp(-total))
-            xc[rs, ns] = x
-            if n < parts:
-                xdt[rs, ns] = (x * scales[rs, 0:LANES]).astype(BF16)
-                xtail[rs, ns] = (x * scales[rs, LANES : 2 * LANES]).astype(BF16)
-                if r + step_rows < span:
-                    ecs[rs, ns] = scales[rs, 2 * LANES :]
-                else:
-                    ecs[r : span - 8, ns] = scales[r : span - 8, 2 * LANES :]
+    for ns in bc_tiles:
+        conv(ns, 0, None)
+    for ns, scales in tiles:
+        conv(ns, 0, scales)
 
     b_t = xc[:, inner : inner + states].T.astype(BF16)
     c_b = xc[:, inner + states : wide].astype(BF16)
@@ -330,20 +342,32 @@
         return remote(g_out.at[i], g_in.at[i], g_send.at[i], g_recv.at[i], cc, t)
 
     def share(i):
-        j = odd * half + i
+        j = odd * 2 * half + i
         return remote(p_out.at[i], st_in.at[j], p_send.at[i], p_recv.at[i], pair, t)
 
     def shared(i):
-        j = (1 - odd) * half + i
+        j = (1 - odd) * 2 * half + i
         return remote(p_out.at[i], st_in.at[j], p_send.at[i], p_recv.at[i], pair, t)
 
     theirs_end = dot(b_t, xtail[:, theirs]).astype(BF16)
+    low = states // 2
+    pieces = 2 * half
+
+    def cut_up(whole):
+        for i in range(pieces):
+            yield whole[(i % 2) * low : (i % 2 + 1) * low, i // 2 * LANES : (i // 2 + 1) * LANES]
+
+    for i, piece in enumerate(cut_up(theirs_end)):
+        x_out[i] = piece
+        end_swap(i).start()
     for i in range(half):
-        x_out[i] = theirs_end[:, i * LANES : (i + 1) * LANES]
-        end_swap(i).start()
+        n = odd * half + i
+        scales = dot(wide_b, spread[n])
+        for r in range(0, span, step_rows):
+            conv(cols(n, LANES), r, scales)
     mine_end = dot(b_t, xtail[:, cols(odd, inner // 2)])
-    for i in range(half):
-        end[i] = mine_end[:, i * LANES : (i + 1) * LANES]
+    for i, piece in enumerate(cut_up(mine_end)):
+        end[i] = piece
     later = lax.broadcasted_iota(jnp.int32, (span, span), 0)
     earlier = lax.broadcasted_iota(jnp.int32, (span, span), 1)
     score[...] = jnp.where(later >= earlier, dot(c_b, b_t), 0.0)
@@ -351,8 +375,8 @@
 
     def relay():
         def part_of(i, _):
-            ls = cols(i, LANES)
-            mine = ecs[span - 8 : span, cols(odd * half + i, LANES)][7:8, :]
+            ls = cols(i // 2, LANES)
+            mine = ecs[span - 8 : span, cols(odd * half + i // 2, LANES)][7:8, :]
             other = pair_decay[:, ls][7:8, :]
             end_swap(i).wait_recv()
             end_mine = end[i]
@@ -375,10 +399,10 @@
 
             p_out[i] = jnp.where(even, second, first).astype(BF16)
             share(i).start()
-            st_in[odd * half + i] = jnp.where(even, first, second).astype(BF16)
+            st_in[odd * pieces + i] = jnp.where(even, first, second).astype(BF16)
             return 0
 
-        lax.fori_loop(0, half, part_of, 0)
+        lax.fori_loop(0, pieces, part_of, 0)
 
     @pl.when(c < 2)
     def _():
@@ -417,14 +441,16 @@
 
     def finish_heads(j):
         ls = cols(j, LANES)
-        y = yb[:, ls] + ecs[:, ls] * dot(c_b, st_in[j])
+        state = st_in[pl.ds(2 * j, 2)].reshape(states, LANES)
+        y = yb[:, ls] + ecs[:, ls] * dot(c_b, state)
         mean_sq = dot(jnp.concatenate(split(y * y, 2), axis=1), same)
         normed[:, ls] = (y * lax.rsqrt(mean_sq + 1e-5) * gain[:, ls]).astype(BF16)
 
     for i in range(half):
         finish_heads(odd * half + i)
     for i in range(half):
-        shared(i).wait_recv()
+        shared(2 * i).wait_recv()
+        shared(2 * i + 1).wait_recv()
         finish_heads((1 - odd) * half + i)
 
     load_out.wait()
@@ -489,7 +515,7 @@
         share(i).wait_send()
         return 0
 
-    lax.fori_loop(0, half, drain_s, 0)
+    lax.fori_loop(0, pieces, drain_s, 0)
 
     @pl.when(has_next)
     def _():
@@ -501,7 +527,7 @@
             hand_down(i, c + 2).wait_send()
             return 0
 
-        lax.fori_loop(0, half, drain_g, 0)
+        lax.fori_loop(0, pieces, drain_g, 0)
 
 
 def per_device(
@@ -541,13 +567,13 @@
             pltpu.VMEM((parts, 8 * heads, 3 * LANES), BF16),
             pltpu.VMEM((span, inner), F32),
             pltpu.VMEM((span, span), F32),
-            pltpu.VMEM((half, states, LANES), F32),
-            pltpu.VMEM((parts, states, LANES), BF16),
-            pltpu.VMEM((half, states, LANES), BF16),
-            pltpu.VMEM((half, states, LANES), BF16),
-            pltpu.VMEM((half, states, LANES), BF16),
-            pltpu.VMEM((half, states, LANES), BF16),
-            pltpu.VMEM((half, states, LANES), BF16),
+            pltpu.VMEM((2 * half, states // 2, LANES), F32),
+            pltpu.VMEM((2 * parts, states // 2, LANES), BF16),
+            pltpu.VMEM((2 * half, states // 2, LANES), BF16),
+            pltpu.VMEM((2 * half, states // 2, LANES), BF16),
+            pltpu.VMEM((2 * half, states // 2, LANES), BF16),
+            pltpu.VMEM((2 * half, states // 2, LANES), BF16),
+            pltpu.VMEM((2 * half, states // 2, LANES), BF16),
             pltpu.VMEM((8, inner // 2), F32),
             pltpu.VMEM((span, inner), BF16),
             pltpu.VMEM((4, rows, oc), F32),
@@ -566,12 +592,12 @@
             dma((K_PARTS,)),
             dma((2,)),
             dma((2,)),
-            dma((half,)),
-            dma((half,)),
-            dma((half,)),
-            dma((half,)),
-            dma((half,)),
-            dma((half,)),
+            dma((2 * half,)),
+            dma((2 * half,)),
+            dma((2 * half,)),
+            dma((2 * half,)),
+            dma((2 * half,)),
+            dma((2 * half,)),
             dma((OUT_PARTS,)),
             dma((OUT_PARTS,)),
             dma((OUT_PARTS,)),

time: 58.5 us -> 56.3 us (0.962)
  Pallas kernels: 56.4 us -> 54.3 us
    pallas_call x1, Pallas kernels: 56.4 us -> 54.3 us  [per_device(): pl.pallas_call(functools.partial(layer_kernel, ctx_size), out_shape=jax.S...]
where the time goes in v4:
time: 56.3 us; the launch traced here: 56.1 us
  Pallas kernels  54.3 us (96%)
  local copies, waits for them, and re-layouts  1.87 us (3%)
    pallas_call x1, Pallas kernels, per_device(): pl.pallas_call(functools.partial(layer_kernel, ctx_size), out_shape=jax.S...  54.3 us
    unnamed x1, local copies, waits for them, and re-layouts  1.87 us

profile of v4, /device:TPU:31, one launch (start us, length us, event | category | flops | bytes accessed | tf_op | source)
XLA Modules:
  0.0 56.1 jit_solution(2843992404679816461)
XLA Ops:
  0.0 54.3 %shard_map.109 = bf16[64,4096]{1,0:T(8,128)(2,1)} custom-call(bf16[64,4096]{1,0:T(8,128)(2,1)} %tokens.1, bf16[4096,1024]{1,0:T(8,128)(2,1)} %in_x.1, bf16[4096,256]{1,0:T(8,128)(2,1)} %in_bc.1, bf16[16,4096]{1,0:T(8,128)(2,1)} %bitcast.5, bf16[1024,4096]{1,0:T(8,128)(2,1)} %out_w.1, f32[4,1024]{1,0:T(4,128)} %conv_x.1, f32[4,256]{1,0:T(4,128)} %conv_bc.1, ...), custom_call_target="tpu_custom_call" | custom-call | tf_op jit(solution)/shard_map/pallas_call | solution.py:548
  54.3 1.9 %copy.13 = bf16[64,4096]{1,0:T(8,128)(2,1)} copy(bf16[64,4096]{1,0:T(8,128)(2,1)} %shard_map.109) | data formatting | bytes 1048576

commit v5 on v4

--- a/solution.py
+++ b/solution.py
@@ -14,6 +14,7 @@
 OUT_PARTS = 16
 TILE = 256
 LANES = 128
+LAG = 2
 
 
 def dot(a, b):
@@ -38,11 +39,16 @@
     out_w,
     conv_x,
     conv_bc,
+    dt_bias_in,
+    a_log_in,
+    skip_d_in,
+    gain_in,
+    out,
     dt_bias,
     a_log,
     skip_d,
     gain,
-    out,
+    staged,
     gath,
     w_in,
     w_dt,
@@ -74,6 +80,8 @@
     recv1,
     send2,
     recv2,
+    small_sem,
+    out_sem,
     load_sem,
     tok_sem,
     a_send,
@@ -106,7 +114,7 @@
     bc = in_bc.shape[1]
     wide = inner + bc
     states = bc // 2
-    heads = dt_bias.shape[1]
+    heads = dt_bias_in.shape[1]
     kc = depth // K_PARTS
     oc = depth // OUT_PARTS
     has_prev = c > 0
@@ -186,6 +194,21 @@
 
     load_tok.start()
     load_dt.start()
+    small = [
+        pltpu.make_async_copy(src, dst, small_sem.at[i])
+        for i, (src, dst) in enumerate(
+            (
+                (conv_x, taps.at[:, 0:inner]),
+                (conv_bc, taps.at[:, inner:wide]),
+                (dt_bias_in, dt_bias),
+                (a_log_in, a_log),
+                (skip_d_in, skip_d),
+                (gain_in, gain),
+            )
+        )
+    ]
+    for copy in small:
+        copy.start()
     for k in range(K_PARTS):
         for copy in load(k):
             copy.start()
@@ -200,8 +223,6 @@
     for k in range(K_PARTS):
         copy_b(k).start()
 
-    taps[:, 0:inner] = conv_x[...]
-    taps[:, inner:wide] = conv_bc[...]
     acc[...] = jnp.zeros_like(acc)
     acc_dt[...] = jnp.zeros_like(acc_dt)
 
@@ -231,6 +252,8 @@
     def upright(row):
         return jnp.sum(jnp.where(eye, row, 0.0), axis=1, keepdims=True)
 
+    for copy in small:
+        copy.wait()
     bias = upright(dt_bias[...])
     rate = -jnp.exp(upright(a_log[...]))
     skip_col = jnp.broadcast_to(upright(skip_d[...]), (heads, LANES))
@@ -238,10 +261,12 @@
     load_tok.wait()
     load_dt.wait()
 
-    def project(k, _):
-        ks = cols(k, kc)
+    def forward(k):
         got(across, k, a_send, a_recv).wait_recv()
         copy_f(k).start()
+
+    def project(k):
+        ks = cols(k, kc)
         got(mate, k, b_send, b_recv).wait_recv()
         for copy in load(k):
             copy.wait()
@@ -254,9 +279,15 @@
         for n in range(wide // TILE):
             ns = slice(n * TILE, (n + 1) * TILE)
             acc[:, ns] += dot(lhs, w_in[ks, ns])
+
+    def gather_step(k, _):
+        forward(k)
+        project(k - 1)
         return 0
 
-    lax.fori_loop(0, K_PARTS, project, 0)
+    forward(0)
+    lax.fori_loop(1, K_PARTS, gather_step, 0)
+    project(K_PARTS - 1)
     load_out.start()
 
     ext[span : span + 8, :] = acc[span - 8 : span, :].astype(BF16).astype(F32)
@@ -303,7 +334,8 @@
         total = taps[0:1, ns] * ext[5 + r : 5 + r + step_rows, ns]
         for k in range(1, 4):
             total = total + taps[k : k + 1, ns] * ext[5 + k + r : 5 + k + r + step_rows, ns]
-        x = total / (1.0 + jnp.exp(-total))
+        x = 0.5 * total
+        x = x * jnp.tanh(x) + x
         xc[rs, ns] = x
         if scales is not None:
             xdt[rs, ns] = (x * scales[rs, 0:LANES]).astype(BF16)
@@ -475,20 +507,26 @@
         send2[j] = (own[j, 0] + recv1[j, 0].astype(F32)).astype(BF16)
         hop2(j).start()
 
-    multiply(0)
+    for j in range(LAG):
+        multiply(j)
 
     def step(j, _):
         multiply(j)
-        pass_on(j - 1)
+        pass_on(j - LAG)
         return 0
 
-    lax.fori_loop(1, OUT_PARTS, step, 0)
-    pass_on(OUT_PARTS - 1)
+    lax.fori_loop(LAG, OUT_PARTS, step, 0)
+    for j in range(OUT_PARTS - LAG, OUT_PARTS):
+        pass_on(j)
+
+    def store(j):
+        return pltpu.make_async_copy(staged.at[j], out.at[:, cols(j, oc)], out_sem.at[j])
 
     def finish(j, _):
         hop2(j).wait_recv()
         total = own[j, 1] + recv1[j, 1].astype(F32) + recv2[j].astype(F32)
-        out[:, cols(j, oc)] = total.astype(BF16)
+        staged[j] = total.astype(BF16)
+        store(j).start()
         return 0
 
     lax.fori_loop(0, OUT_PARTS, finish, 0)
@@ -504,6 +542,7 @@
     def drain_o(j, _):
         hop1(j).wait_send()
         hop2(j).wait_send()
+        store(j).wait()
         return 0
 
     lax.fori_loop(0, OUT_PARTS, drain_o, 0)
@@ -544,13 +583,17 @@
     oc = depth // OUT_PARTS
     dma = pltpu.SemaphoreType.DMA
     anywhere = pl.BlockSpec(memory_space=pl.ANY)
-    local = pl.BlockSpec(memory_space=pltpu.VMEM)
     return pl.pallas_call(
         functools.partial(layer_kernel, ctx_size),
         out_shape=jax.ShapeDtypeStruct((rows, depth), BF16),
-        in_specs=[anywhere] * 5 + [local] * 6,
-        out_specs=local,
+        in_specs=[anywhere] * 11,
+        out_specs=anywhere,
         scratch_shapes=[
+            pltpu.VMEM((1, heads), F32),
+            pltpu.VMEM((1, heads), F32),
+            pltpu.VMEM((1, heads), F32),
+            pltpu.VMEM((1, inner), F32),
+            pltpu.VMEM((OUT_PARTS, rows, oc), BF16),
             pltpu.VMEM((4, rows, depth), BF16),
             pltpu.VMEM((depth, wide), BF16),
             pltpu.VMEM((heads, depth), BF16),
@@ -582,6 +625,8 @@
             pltpu.VMEM((OUT_PARTS, 2, rows, oc), BF16),
             pltpu.VMEM((OUT_PARTS, rows, oc), BF16),
             pltpu.VMEM((OUT_PARTS, rows, oc), BF16),
+            dma((6,)),
+            dma((OUT_PARTS,)),
             dma((3, K_PARTS)),
             dma(()),
             dma((K_PARTS,)),

time: 56.3 us -> 53.5 us (0.950)
  Pallas kernels: 54.3 us -> 51.5 us
    pallas_call x1, Pallas kernels: 54.3 us -> 51.5 us  [per_device(): pl.pallas_call(functools.partial(layer_kernel, ctx_size), out_shape=jax.S...]
where the time goes in v5:
time: 53.5 us; the launch traced here: 53.4 us
  Pallas kernels  51.5 us (96%)
  local copies, waits for them, and re-layouts  1.87 us (3%)
    pallas_call x1, Pallas kernels, per_device(): pl.pallas_call(functools.partial(layer_kernel, ctx_size), out_shape=jax.S...  51.5 us
    unnamed x1, local copies, waits for them, and re-layouts  1.87 us

profile of v5, /device:TPU:31, one launch (start us, length us, event | category | flops | bytes accessed | tf_op | source)
XLA Modules:
  0.0 53.4 jit_solution(10736361606091067458)
XLA Ops:
  0.0 51.5 %shard_map.109 = bf16[64,4096]{1,0:T(8,128)(2,1)} custom-call(bf16[64,4096]{1,0:T(8,128)(2,1)} %tokens.1, bf16[4096,1024]{1,0:T(8,128)(2,1)} %in_x.1, bf16[4096,256]{1,0:T(8,128)(2,1)} %in_bc.1, bf16[16,4096]{1,0:T(8,128)(2,1)} %bitcast.5, bf16[1024,4096]{1,0:T(8,128)(2,1)} %out_w.1, f32[4,1024]{1,0:T(4,128)} %conv_x.1, f32[4,256]{1,0:T(4,128)} %conv_bc.1, ...), custom_call_target="tpu_custom_call" | custom-call | tf_op jit(solution)/shard_map/pallas_call | solution.py:586
  51.5 1.9 %copy.13 = bf16[64,4096]{1,0:T(8,128)(2,1)} copy(bf16[64,4096]{1,0:T(8,128)(2,1)} %shard_map.109) | data formatting | bytes 1048576

commit v6 on v5

--- a/solution.py
+++ b/solution.py
@@ -14,7 +14,6 @@
 OUT_PARTS = 16
 TILE = 256
 LANES = 128
-LAG = 2
 
 
 def dot(a, b):
@@ -74,7 +73,7 @@
     p_out,
     pair_decay,
     normed,
-    part,
+    ordered,
     own,
     send1,
     recv1,
@@ -405,36 +404,36 @@
     score[...] = jnp.where(later >= earlier, dot(c_b, b_t), 0.0)
     decay_swap.wait_recv()
 
+    def relay_piece(i, _):
+        ls = cols(i // 2, LANES)
+        mine = ecs[span - 8 : span, cols(odd * half + i // 2, LANES)][7:8, :]
+        other = pair_decay[:, ls][7:8, :]
+        end_swap(i).wait_recv()
+        end_mine = end[i]
+        end_other = x_in[i].astype(F32)
+
+        @pl.when(has_prev2)
+        def _():
+            hand_down(i, c - 2).wait_recv()
+
+        even = odd == 0
+        first = g_in[i].astype(F32)
+        second = jnp.where(even, mine, other) * first + jnp.where(even, end_mine, end_other)
+
+        @pl.when(has_next2)
+        def _():
+            after = jnp.where(even, other, mine) * second
+            after = after + jnp.where(even, end_other, end_mine)
+            g_out[i] = after.astype(BF16)
+            hand_down(i, c + 2).start()
+
+        p_out[i] = jnp.where(even, second, first).astype(BF16)
+        share(i).start()
+        st_in[odd * pieces + i] = jnp.where(even, first, second).astype(BF16)
+        return 0
+
     def relay():
-        def part_of(i, _):
-            ls = cols(i // 2, LANES)
-            mine = ecs[span - 8 : span, cols(odd * half + i // 2, LANES)][7:8, :]
-            other = pair_decay[:, ls][7:8, :]
-            end_swap(i).wait_recv()
-            end_mine = end[i]
-            end_other = x_in[i].astype(F32)
-
-            @pl.when(has_prev2)
-            def _():
-                hand_down(i, c - 2).wait_recv()
-
-            even = odd == 0
-            first = g_in[i].astype(F32)
-            second = jnp.where(even, mine, other) * first + jnp.where(even, end_mine, end_other)
-
-            @pl.when(has_next2)
-            def _():
-                after = jnp.where(even, other, mine) * second
-                after = after + jnp.where(even, end_other, end_mine)
-                g_out[i] = after.astype(BF16)
-                hand_down(i, c + 2).start()
-
-            p_out[i] = jnp.where(even, second, first).astype(BF16)
-            share(i).start()
-            st_in[odd * pieces + i] = jnp.where(even, first, second).astype(BF16)
-            return 0
-
-        lax.fori_loop(0, pieces, part_of, 0)
+        lax.fori_loop(0, pieces, relay_piece, 0)
 
     @pl.when(c < 2)
     def _():
@@ -461,10 +460,6 @@
             skip = jnp.where(low_row, skip_col[2 * j : 2 * j + 1], skip_col[2 * j + 1 : 2 * j + 2])
             yb[rs, ls] = jnp.where(low_head, both[0], both[1]) + skip * xc[rs, ls]
 
-    @pl.when(c >= 4)
-    def _():
-        relay()
-
     same = (
         lax.broadcasted_iota(jnp.int32, (2 * LANES, LANES), 0) % LANES // head_width
         == lax.broadcasted_iota(jnp.int32, (2 * LANES, LANES), 1) // head_width
@@ -478,8 +473,28 @@
         mean_sq = dot(jnp.concatenate(split(y * y, 2), axis=1), same)
         normed[:, ls] = (y * lax.rsqrt(mean_sq + 1e-5) * gain[:, ls]).astype(BF16)
 
-    for i in range(half):
-        finish_heads(odd * half + i)
+    @pl.when((c >= 4) & has_next2)
+    def _():
+        relay()
+
+    at_end = (c >= 4) & (c >= ctx_size - 2)
+
+    @pl.when(at_end)
+    def _():
+        def tile_of(i, _):
+            relay_piece(2 * i, 0)
+            relay_piece(2 * i + 1, 0)
+            finish_heads(odd * half + i)
+            return 0
+
+        lax.fori_loop(0, half, tile_of, 0)
+
+
+    @pl.when(jnp.logical_not(at_end))
+    def _():
+        for i in range(half):
+            finish_heads(odd * half + i)
+
     for i in range(half):
         shared(2 * i).wait_recv()
         shared(2 * i + 1).wait_recv()
@@ -493,31 +508,38 @@
     def hop2(j):
         return remote(send2.at[j], recv2.at[j], r2_send.at[j], r2_recv.at[j], c, across)
 
+    def block(b):
+        return normed[pl.ds(pl.multiple_of(b * rows, rows), rows), :]
+
+    for at, b in enumerate((far, mate, across, t)):
+        ordered[at * rows : (at + 1) * rows, :] = block(b)
+
     def multiply(j):
-        prod = dot(normed[...], w_out[:, cols(j, oc)])
-        part[...] = prod.reshape(4, rows, oc)
-        send1[j, 0] = part[far].astype(BF16)
-        send1[j, 1] = part[mate].astype(BF16)
-        hop1(j).start()
-        own[j, 0] = part[across]
-        own[j, 1] = part[t]
+        prod = dot(ordered[...], w_out[:, cols(j, 2 * oc)])
+        for u in range(2):
+            cut_at = slice(u * oc, (u + 1) * oc)
+            out_rows = prod[: 2 * rows, cut_at].astype(BF16)
+            send1[2 * j + u] = out_rows.reshape(2, rows, oc)
+            hop1(2 * j + u).start()
+        for u in range(2):
+            own[2 * j + u] = prod[2 * rows :, u * oc : (u + 1) * oc].reshape(2, rows, oc)
 
     def pass_on(j):
         hop1(j).wait_recv()
         send2[j] = (own[j, 0] + recv1[j, 0].astype(F32)).astype(BF16)
         hop2(j).start()
 
-    for j in range(LAG):
-        multiply(j)
+    multiply(0)
 
     def step(j, _):
         multiply(j)
-        pass_on(j - LAG)
+        pass_on(2 * j - 2)
+        pass_on(2 * j - 1)
         return 0
 
-    lax.fori_loop(LAG, OUT_PARTS, step, 0)
-    for j in range(OUT_PARTS - LAG, OUT_PARTS):
-        pass_on(j)
+    lax.fori_loop(1, OUT_PARTS // 2, step, 0)
+    pass_on(OUT_PARTS - 2)
+    pass_on(OUT_PARTS - 1)
 
     def store(j):
         return pltpu.make_async_copy(staged.at[j], out.at[:, cols(j, oc)], out_sem.at[j])
@@ -619,7 +641,7 @@
             pltpu.VMEM((2 * half, states // 2, LANES), BF16),
             pltpu.VMEM((8, inner // 2), F32),
             pltpu.VMEM((span, inner), BF16),
-            pltpu.VMEM((4, rows, oc), F32),
+            pltpu.VMEM((span, inner), BF16),
             pltpu.VMEM((OUT_PARTS, 2, rows, oc), F32),
             pltpu.VMEM((OUT_PARTS, 2, rows, oc), BF16),
             pltpu.VMEM((OUT_PARTS, 2, rows, oc), BF16),

time: 53.5 us -> 53.5 us (level)
  no operation moved by 1% of the time
where the time goes in v6:
time: 53.5 us; the launch traced here: 53.4 us
  Pallas kernels  51.5 us (96%)
  local copies, waits for them, and re-layouts  1.87 us (3%)
    pallas_call x1, Pallas kernels, per_device(): pl.pallas_call(functools.partial(layer_kernel, ctx_size), out_shape=jax.S...  51.5 us
    unnamed x1, local copies, waits for them, and re-layouts  1.87 us

profile of v6, /device:TPU:31, one launch (start us, length us, event | category | flops | bytes accessed | tf_op | source)
XLA Modules:
  0.0 53.4 jit_solution(3720937634052232004)
XLA Ops:
  0.0 51.5 %shard_map.109 = bf16[64,4096]{1,0:T(8,128)(2,1)} custom-call(bf16[64,4096]{1,0:T(8,128)(2,1)} %tokens.1, bf16[4096,1024]{1,0:T(8,128)(2,1)} %in_x.1, bf16[4096,256]{1,0:T(8,128)(2,1)} %in_bc.1, bf16[16,4096]{1,0:T(8,128)(2,1)} %bitcast.5, bf16[1024,4096]{1,0:T(8,128)(2,1)} %out_w.1, f32[4,1024]{1,0:T(4,128)} %conv_x.1, f32[4,256]{1,0:T(4,128)} %conv_bc.1, ...), custom_call_target="tpu_custom_call" | custom-call | tf_op jit(solution)/shard_map/pallas_call | solution.py:608
  51.5 1.9 %copy.13 = bf16[64,4096]{1,0:T(8,128)(2,1)} copy(bf16[64,4096]{1,0:T(8,128)(2,1)} %shard_map.109) | data formatting | bytes 1048576

commit v7 on v6

--- a/solution.py
+++ b/solution.py
@@ -433,7 +433,7 @@
         return 0
 
     def relay():
-        lax.fori_loop(0, pieces, relay_piece, 0)
+        lax.fori_loop(0, pieces, relay_piece, 0, unroll=4)
 
     @pl.when(c < 2)
     def _():

time: 53.5 us -> 53.5 us (level)
  no operation moved by 1% of the time
where the time goes in v7:
time: 53.5 us; the launch traced here: 53.4 us
  Pallas kernels  51.5 us (96%)
  local copies, waits for them, and re-layouts  1.87 us (3%)
    pallas_call x1, Pallas kernels, per_device(): pl.pallas_call(functools.partial(layer_kernel, ctx_size), out_shape=jax.S...  51.5 us
    unnamed x1, local copies, waits for them, and re-layouts  1.87 us

profile of v7, /device:TPU:31, one launch (start us, length us, event | category | flops | bytes accessed | tf_op | source)
XLA Modules:
  0.0 53.4 jit_solution(8269710736757657996)
XLA Ops:
  0.0 51.5 %shard_map.109 = bf16[64,4096]{1,0:T(8,128)(2,1)} custom-call(bf16[64,4096]{1,0:T(8,128)(2,1)} %tokens.1, bf16[4096,1024]{1,0:T(8,128)(2,1)} %in_x.1, bf16[4096,256]{1,0:T(8,128)(2,1)} %in_bc.1, bf16[16,4096]{1,0:T(8,128)(2,1)} %bitcast.5, bf16[1024,4096]{1,0:T(8,128)(2,1)} %out_w.1, f32[4,1024]{1,0:T(4,128)} %conv_x.1, f32[4,256]{1,0:T(4,128)} %conv_bc.1, ...), custom_call_target="tpu_custom_call" | custom-call | tf_op jit(solution)/shard_map/pallas_call | solution.py:608
  51.5 1.9 %copy.13 = bf16[64,4096]{1,0:T(8,128)(2,1)} copy(bf16[64,4096]{1,0:T(8,128)(2,1)} %shard_map.109) | data formatting | bytes 1048576
